TPU v7x, 512 devices: a whole 4x4x16 slice. The times are simulated.
512 devices in a mesh: grp: 32 (over x_lo, z), seq: 16 (over x_hi, y, core).
Axes of the slice: x: 4 (x_hi: 2, x_lo: 2; x = x_hi * 2 + x_lo), y: 4, z: 16, core: 2. Of those that a mesh axis runs over, the one named last changes fastest.
Arguments:
- cache: bfloat16 [512, 3584, 576], P(('grp', 'seq')), parts along dimension 0, may hold values from -12 to 12
- lengths: int32 [128], P('grp'), parts along dimension 0, may hold values from 896 to 3584, as said below
- owners: int32 [128], P('grp'), parts along dimension 0, may hold values from 0 to 15, as said below
- positions: int32 [128, 12], P('grp'), parts along dimension 0, may hold values from 0 to 11, as said below
- q_nope: bfloat16 [128, 12, 8192], P('grp', None, 'seq'), parts along dimension 0, may hold values from -6 to 6
- q_rope: bfloat16 [128, 12, 4096], P('grp', None, 'seq'), parts along dimension 0, may hold values from -12 to 12
- absorb_weight: bfloat16 [64, 128, 512], P('seq'), may hold values from -0.5 to 0.5
- new_latent: bfloat16 [128, 12, 576], P('grp'), parts along dimension 0, may hold values from -15 to 15
Outputs:
- attn_latent: bfloat16 [128, 12, 32768], P('grp', None, 'seq'), parts along dimension 0
There are 32 independent parts, one for each index of `grp`. A program takes and returns all parts, laid end to end along the dimension named above; an argument that names none is the same for every part. Nothing has to cross between parts.
Inputs may be any that keep to these rules, and one draw needn't show every extreme that they name: `lengths`: one straggler has the full length 3584. The owners of a group are distinct ranks. Step j's tokens have consecutive positions b_j, b_j + 1, b_j + 2 with b_0 = 0 and b_j - b_(j-1) between 1 and 3.
All inputs are finite; a program needn't handle non-finite values.
Results may differ from a plain program's by a relative error of at most 0.015.
Values may be sent and summed in bfloat16 or wider, within the bound.
No kernel may reach another device: no remote copies, remote signals or barrier semaphores. Data moves between devices by JAX's collectives and lax.ppermute only.
A program may use at most 64 MiB of HBM per device.

v0:
```python
import math

import jax
import jax.numpy as jnp
from jax import lax
from jax.sharding import PartitionSpec as P

KVL = 512
ROPE = 64
NOPE = 128


def shards(cache, lengths, owners, positions, q_nope, q_rope, absorb_weight, new_latent):
    piece_count = lax.axis_size("seq")
    my_index = lax.axis_index("seq")
    strag_count = q_nope.shape[0]
    tok_count = q_nope.shape[1]
    heads_dev = absorb_weight.shape[0]
    ctx_rows = cache.shape[1]
    latent_width = cache.shape[2]
    piece_rows = ctx_rows // piece_count
    score_scale = 1.0 / math.sqrt(NOPE + ROPE)
    query_nope = q_nope.reshape(strag_count, tok_count, heads_dev, NOPE)
    absorbed = jnp.einsum(
        "sthn,hnc->sthc", query_nope, absorb_weight, preferred_element_type=jnp.float32
    ).astype(jnp.bfloat16)
    query_rope = q_rope.reshape(strag_count, tok_count, heads_dev, ROPE)
    local_query = jnp.concatenate([absorbed, query_rope], axis=-1)
    query = lax.all_gather(local_query, "seq", axis=2, tiled=True)
    all_heads = query.shape[2]
    query = query.reshape(strag_count, tok_count * all_heads, latent_width)
    sending = cache.reshape(piece_count, piece_rows, latent_width)
    received = lax.all_to_all(sending, "seq", split_axis=0, concat_axis=0, tiled=True)
    keys_here = jnp.take(received, owners, axis=0)
    raw = (
        jnp.einsum("src,sqc->srq", keys_here, query, preferred_element_type=jnp.float32)
        * score_scale
    )
    scores = raw
    slot_index = my_index * piece_rows + lax.iota(jnp.int32, piece_rows)
    visible = slot_index[None, :, None] < lengths[:, None, None]
    scores = jnp.where(visible, scores, -jnp.inf)
    new_scores = (
        jnp.einsum("sqc,skc->sqk", query, new_latent, preferred_element_type=jnp.float32)
        * score_scale
    )
    query_pos = jnp.repeat(positions, all_heads, axis=1)
    new_seen = (positions[:, None, :] <= query_pos[:, :, None]) & (my_index == 0)
    new_scores = jnp.where(new_seen, new_scores, -jnp.inf)
    local_top = jnp.maximum(jnp.max(scores, axis=1), jnp.max(new_scores, axis=-1))
    row_top = lax.pmax(local_top, "seq")
    weights = jnp.where(visible, jnp.exp(scores - row_top[:, None, :]), 0.0)
    new_weights = jnp.where(new_seen, jnp.exp(new_scores - row_top[:, :, None]), 0.0)
    local_total = jnp.sum(weights, axis=1) + jnp.sum(new_weights, axis=-1)
    partial_value = jnp.einsum(
        "srq,src->sqc",
        weights.astype(jnp.bfloat16),
        keys_here[:, :, :KVL],
        preferred_element_type=jnp.float32,
    )
    new_part = jnp.einsum(
        "sqk,skc->sqc",
        new_weights.astype(jnp.bfloat16),
        new_latent[:, :, :KVL],
        preferred_element_type=jnp.float32,
    )
    partial_value = (partial_value + new_part).astype(jnp.bfloat16).astype(jnp.float32)
    partial_value = partial_value.reshape(strag_count, tok_count, all_heads * KVL)
    total = lax.psum(local_total, "seq")
    total = total.reshape(strag_count, tok_count, all_heads)
    total = lax.dynamic_slice_in_dim(total, my_index * heads_dev, heads_dev, 2)
    summed = lax.psum_scatter(
        partial_value.astype(jnp.bfloat16), "seq", scatter_dimension=2, tiled=True
    ).astype(jnp.float32)
    summed = summed.reshape(strag_count, tok_count, heads_dev, KVL)
    result = (summed / total[:, :, :, None]).astype(jnp.bfloat16)
    return result.reshape(strag_count, tok_count, heads_dev * KVL)


def solution(mesh):
    in_specs = (
        P(("grp", "seq"), None, None),
        P("grp"),
        P("grp"),
        P("grp", None),
        P("grp", None, "seq"),
        P("grp", None, "seq"),
        P("seq", None, None),
        P("grp", None, None),
    )
    out_specs = P("grp", None, "seq")
    return jax.shard_map(shards, mesh=mesh, in_specs=in_specs, out_specs=out_specs, check_vma=False)
```

profile of v0, /device:TPU:1, one launch (start us, length us, event | category | flops | bytes accessed | tf_op | source)
XLA Modules:
  0.0 309.8 jit_solution(17927123407364998245)
XLA Ops:
  6.5 0.0 copy-start
  6.5 0.0 all-gather.2.cloned.1.call-start
  6.5 0.9 reshape.69
  7.5 0.8 reshape.68
  8.3 0.0 copy-done
  8.3 0.2 fusion.10
  8.6 0.8 copy.36
  9.4 0.0 all-gather.2.cloned.1.call-update
  9.4 6.6 %copy.48 = bf16[1,3584,576]{2,1,0:T(8,128)(2,1)} copy(bf16[1,3584,576]{1,2,0:T(8,128)(2,1)} %param.8) | data formatting | bytes 8257536 | tf_op jit(solution)/shard_map/reshape | solution.py:32
  16.0 0.0 copy-start.4
  16.0 0.0 copy-start.2
  16.0 0.0 copy-start.6
  16.0 0.0 copy-start.5
  16.0 11.3 %all-to-all-start = ((bf16[16,224,576]{2,1,0:T(8,128)(2,1)}), bf16[16,224,576]{2,1,0:T(8,128)(2,1)}, u32[]{:S(2)}, u32[]{:S(2)}) async-start(bf16[16,224,576]{2,1,0:T(8,128)(2,1)} %bitcast.18), calls=%async_computation | async-start | bytes 9175040 | tf_op jit(solution)/shard_map/all_to_all | solution.py:33
  27.3 0.0 reduce-scatter.2.cloned.1.call-start
  27.3 0.0 copy-done.4
  27.3 0.1 broadcast_in_dim.51
  27.4 0.1 le.22
  27.5 0.0 copy-done.2
  27.5 0.7 copy.40
  28.2 0.0 copy-done.6
  28.2 0.0 copy-done.5
  28.2 0.1 broadcast_compare_fusion
  28.3 61.0 %all-to-all-done = bf16[16,224,576]{2,1,0:T(8,128)(2,1)} async-done(((bf16[16,224,576]{2,1,0:T(8,128)(2,1)}), bf16[16,224,576]{2,1,0:T(8,128)(2,1)}, u32[]{:S(2)}, u32[]{:S(2)}) %all-to-all-start) | async-done | bytes 4128800 | tf_op jit(solution)/shard_map/all_to_all | solution.py:33
  89.3 3.1 gather_fusion
  92.3 1.2 broadcast_select_fusion
  93.5 23.7 %all-gather.2.cloned.1.call-done = bf16[4,12,64,576]{3,0,1,2:T(4,128)(2,1)} async-done(((bf16[4,12,4,576]{3,0,1,2:T(4,128)(2,1)}), bf16[4,12,64,576]{3,0,1,2:T(4,128)(2,1)}) %all-gather.2.cloned.1.call-update) | async-done | bytes 3538960 | tf_op jit(solution)/shard_map/all_gather | solution.py:29
  117.2 0.0 copy-start.1
  117.2 3.1 %copy.37 = bf16[4,12,64,576]{3,2,1,0:T(8,128)(2,1)S(1)} copy(bf16[4,12,64,576]{3,0,1,2:T(4,128)(2,1)} %all-gather.2.cloned.1.call-done) | data formatting | bytes 7077888 | tf_op jit(solution)/shard_map/all_gather | solution.py:29
  120.3 0.0 copy-done.1
  120.4 1.5 fusion
  121.9 1.2 fusion.30
  123.0 60.4 %pmax.7 = f32[4,768]{1,0:T(4,128)S(1)} all-reduce(f32[4,768]{1,0:T(4,128)S(1)} %max.5), channel_id=1, replica_groups=mesh['grp'=32,'seq'=16] {'seq'}, use_global_device_ids=true, to_apply=%region_2.3 | all-reduce | flops 3072 | bytes 24576 | tf_op jit(solution)/shard_map/pmax | solution.py:51
  183.4 0.0 copy-start.3
  183.4 2.5 fusion.3
  186.0 0.0 copy-done.3
  186.0 2.8 add_convert_fusion
  188.8 5.4 %convert_element_type.32 = bf16[4,12,32768]{2,1,0:T(8,128)(2,1)} reshape(bf16[4,768,512]{2,1,0:T(8,128)(2,1)} %add_convert_fusion) | data formatting | bytes 6291456 | tf_op jit(solution)/shard_map/convert_element_type | solution.py:73
  194.2 0.0 reduce-scatter.2.cloned.1.call-update
  194.2 0.1 fusion.15
  194.3 0.8 fusion.1
  195.1 0.1 reshape.71
  195.2 65.1 %psum.7 = f32[4,12,64]{2,1,0:T(8,128)S(1)} all-reduce(f32[4,12,64]{2,1,0:T(8,128)S(1)} %reshape.71), channel_id=1, replica_groups=mesh['grp'=32,'seq'=16] {'seq'}, use_global_device_ids=true, to_apply=%region_6.7 | all-reduce | flops 3072 | bytes 24576 | tf_op jit(solution)/shard_map/psum | solution.py:69
  260.3 0.1 constant_dynamic-slice_fusion
  260.4 0.1 div.11
  260.5 0.3 div.12
  260.8 40.1 %reduce-scatter.2.cloned.1.call-done = bf16[4,12,2048]{2,1,0:T(8,128)(2,1)} async-done(((bf16[4,12,32768]{2,1,0:T(8,128)(2,1)}), bf16[4,12,2048]{2,1,0:T(8,128)(2,1)}) %reduce-scatter.2.cloned.1.call-update) | async-done | bytes 196624 | tf_op jit(solution)/shard_map/reduce_scatter | solution.py:72
  300.9 1.2 fusion.14
  302.1 0.8 copy.44
  (9 shorter events, 0.1 us)
Async XLA Ops:
  6.5 1.8 copy-start
  6.5 110.7 %all-gather.2.cloned.1.call-start = ((), (), s32[]{:S(2)}) async-start(), calls=%async_computation.2 | async-start | bytes 4177920 | tf_op jit(solution)/shard_map/all_gather | solution.py:29
  16.0 11.4 %copy-start.4 = (s32[4,12]{1,0:T(4,128)S(1)}, s32[4,12]{1,0:T(4,128)}, u32[]{:S(2)}) copy-start(s32[4,12]{1,0:T(4,128)} %param.11) | copy-start | bytes 580
  16.0 11.5 %copy-start.2 = (bf16[4,12,576]{2,0,1:T(4,128)(2,1)S(1)}, bf16[4,12,576]{2,0,1:T(4,128)(2,1)}, u32[]{:S(2)}) copy-start(bf16[4,12,576]{2,0,1:T(4,128)(2,1)} %param.15) | copy-start | bytes 165892
  16.0 12.2 %copy-start.6 = (s32[4]{0:T(128)S(1)}, s32[4]{0:T(128)}, u32[]{:S(2)}) copy-start(s32[4]{0:T(128)} %param.10) | copy-start | bytes 52
  16.0 12.2 %copy-start.5 = (s32[4]{0:T(128)S(1)}, s32[4]{0:T(128)}, u32[]{:S(2)}) copy-start(s32[4]{0:T(128)} %param.9) | copy-start | bytes 52
  16.0 73.3 %all-to-all-start = ((bf16[16,224,576]{2,1,0:T(8,128)(2,1)}), bf16[16,224,576]{2,1,0:T(8,128)(2,1)}, u32[]{:S(2)}, u32[]{:S(2)}) async-start(bf16[16,224,576]{2,1,0:T(8,128)(2,1)} %bitcast.18), calls=%async_computation | async-start | bytes 9175040 | tf_op jit(solution)/shard_map/all_to_all | solution.py:33
  27.3 273.6 %reduce-scatter.2.cloned.1.call-start = ((), (), s32[]{:S(2)}) async-start(), calls=%async_computation.3 | async-start | bytes 4456448 | tf_op jit(solution)/shard_map/reduce_scatter | solution.py:72
  117.2 3.1 %copy-start.1 = (bf16[4,224,576]{2,1,0:T(8,128)(2,1)S(1)}, bf16[4,224,576]{2,1,0:T(8,128)(2,1)}, u32[]{:S(2)}) copy-start(bf16[4,224,576]{2,1,0:T(8,128)(2,1)} %broadcast_select_fusion) | copy-start | bytes 3096580
  183.4 2.5 copy-start.3
Sparse Core Ops, SparseCore 0:
  10.7 106.4 all-gather.1
  194.3 106.5 reduce-scatter.1
where the time goes:
time: 311 us; the launch traced here: 310 us
  waiting for transfers between devices  125 us (40%)
  blocking collectives  125 us (40%)
  local copies, waits for them, and re-layouts  22.9 us (7%)
  between operations  13.6 us (4%)
  starting transfers between devices  11.3 us (4%)
  matrix products  8.19 us (3%)
  other arithmetic  3.43 us (1%)
    psum x1, blocking collectives, shards(): total = lax.psum(local_total, 'seq')  65.1 us
    all_to_all x1, waiting for transfers between devices, shards(): lax.all_to_all(sending, 'seq', split_axis=0, concat_axis=0, tiled=True)  61 us
    pmax x1, blocking collectives, shards(): row_top = lax.pmax(local_top, 'seq')  60.4 us
    reduce_scatter x1, waiting for transfers between devices, shards(): lax.psum_scatter(partial_value.astype(jnp.bfloat16), 'seq', scatter_dimen...  40.1 us
    all_gather x1, waiting for transfers between devices, shards(): query = lax.all_gather(local_query, 'seq', axis=2, tiled=True)  23.7 us
    all_to_all x1, starting transfers between devices, shards(): lax.all_to_all(sending, 'seq', split_axis=0, concat_axis=0, tiled=True)  11.3 us
    reshape x1, local copies, waits for them, and re-layouts, shards(): sending = cache.reshape(piece_count, piece_rows, latent_width)  6.57 us
  transfers between devices with their start and end apart: 3, of which 3 were waited for; matrix products, arithmetic and copies ran while one was open for 4% of the time, Pallas kernels for 0%

commit v1 on v0

v1 whole, which is shorter than its diff:
```python
import functools
import math

import jax
import jax.numpy as jnp
from jax import lax
from jax.experimental import pallas as pl
from jax.experimental.pallas import tpu as pltpu
from jax.sharding import PartitionSpec as P

KVL = 512
ROPE = 64
NOPE = 128
NEW_PAD = 128
CHUNK = 512
HEAD = NEW_PAD + CHUNK
F32 = jnp.float32
BF16 = jnp.bfloat16
HIDDEN = -1e30
WIDE = 640
VMEM = pltpu.VMEM


def iota2(shape, dim):
    return lax.broadcasted_iota(jnp.int32, shape, dim)


def absorb_kernel(strags, toks, heads, owners_ref, nope_hbm, rope_hbm, weight_hbm, out_hbm, nope_ref, rope_ref, weight_ref, nope_rows, rope_rows, slots, sems, out_sems):
    copies = [
        pltpu.make_async_copy(src, dst, sems.at[i])
        for i, (src, dst) in enumerate(((nope_hbm, nope_ref), (rope_hbm, rope_ref), (weight_hbm, weight_ref)))
    ]
    for copy in copies:
        copy.start()
    rows = strags * toks * heads
    per = toks * heads
    wide = (rows, toks * strags)
    row, col = iota2(wide, 0), iota2(wide, 1)
    pick = (col == (row % per) // heads * strags + row // per).astype(F32).astype(BF16)
    fold = (iota2((heads * ROPE, ROPE), 0) % ROPE == iota2((heads * ROPE, ROPE), 1)).astype(F32).astype(BF16)
    tail = (rows, WIDE - KVL - ROPE)
    marks = (iota2(tail, 1) == iota2(tail, 0) % per // heads).astype(F32).astype(BF16)

    def spread(ref, width):
        copied = jnp.dot(pick, ref[...].astype(BF16), preferred_element_type=F32)
        shape = (rows, heads * width)
        own = iota2(shape, 1) // width == iota2(shape, 0) % heads
        return jnp.where(own, copied, 0.0).astype(BF16)

    copies[0].wait()
    copies[1].wait()
    for t in range(toks):
        nope_rows[t * strags : (t + 1) * strags, :] = nope_ref[t].astype(F32)
        rope_rows[t * strags : (t + 1) * strags, :] = rope_ref[t].astype(F32)
    roped = jnp.dot(spread(rope_rows, ROPE), fold, preferred_element_type=F32).astype(BF16)
    slots[:, KVL:] = jnp.concatenate([roped, marks], axis=1)
    expanded = spread(nope_rows, NOPE)
    copies[2].wait()
    slots[:, :KVL] = jnp.dot(expanded, weight_ref[...], preferred_element_type=F32).astype(BF16)
    leaving = [
        pltpu.make_async_copy(slots.at[pl.ds(s * per, per)], out_hbm.at[owners_ref[s]], out_sems.at[s]) for s in range(strags)
    ]
    for copy in leaving:
        copy.start()
    for copy in leaving:
        copy.wait()


def straggler_here(strags, me_ref, owners_ref):
    mine = jnp.int32(-1)
    for s in range(strags):
        mine = jnp.where(owners_ref[s] == me_ref[0], s, mine)
    return mine


def stage_kernel(strags, me_ref, owners_ref, lengths_ref, new_ref, keys_ref, out_ref, tail, sems):
    mine = straggler_here(strags, me_ref, owners_ref)
    width = keys_ref.shape[0]
    count = out_ref.shape[1] - NEW_PAD

    @pl.when(mine >= 0)
    def _():
        copies = [
            pltpu.make_async_copy(
                keys_ref.at[:, pl.ds(0, count)], out_ref.at[pl.ds(0, width), pl.ds(NEW_PAD, count)], sems.at[0]
            ),
            pltpu.make_async_copy(new_ref.at[mine], out_ref.at[:, pl.ds(0, NEW_PAD)], sems.at[1]),
            pltpu.make_async_copy(tail, out_ref.at[pl.ds(width, WIDE - width), pl.ds(NEW_PAD, count)], sems.at[2]),
        ]
        copies[0].start()
        copies[1].start()
        tail[...] = jnp.where(iota2(tail.shape, 1) < lengths_ref[mine], 0.0, HIDDEN).astype(BF16)
        copies[2].start()
        for copy in copies:
            copy.wait()


def attend_kernel(strags, me_ref, owners_ref, lengths_ref, query_ref, head_ref, keys_ref, out_ref, keys, raw_even, raw_odd, acc, total, top_even, top_odd, answer, key_sems, sem):
    mine = straggler_here(strags, me_ref, owners_ref)
    width, ctx = keys_ref.shape
    count = ctx // CHUNK
    factor = math.log2(math.e) / math.sqrt(NOPE + ROPE)

    def key_copy(i):
        part = pl.ds(pl.multiple_of(i * CHUNK, CHUNK), CHUNK)
        return pltpu.make_async_copy(keys_ref.at[:, part], keys.at[pl.ds(0, width), part], key_sems.at[i])

    def score(keys_part, raw, size, top_before, top_after):
        part = jnp.dot(query_ref[...], keys_part, preferred_element_type=F32)
        raw[:, :size] = part
        peak = part[:, :128]
        for j in range(128, size, 128):
            peak = jnp.maximum(peak, part[:, j : j + 128])
        peak = jnp.broadcast_to(jnp.max(peak, axis=1, keepdims=True), peak.shape)
        top_after[...] = peak if top_before is None else jnp.maximum(top_before[...], peak)

    def weigh(values_part, raw, size, top_before, top_after):
        top = top_after[...]
        shift = top * factor
        pieces = [jnp.exp2(raw[:, j : j + 128] * factor - shift) for j in range(0, size, 128)]
        mass = pieces[0]
        for piece in pieces[1:]:
            mass = mass + piece
        weight = pieces[0] if size == 128 else jnp.concatenate(pieces, axis=1)
        value = lax.dot_general(weight.astype(BF16), values_part, (((1,), (1,)), ((), ())), preferred_element_type=F32)
        if top_before is None:
            total[...] = mass
            acc[...] = value
            return
        fade = jnp.exp2(top_before * factor - shift)
        total[...] = total[...] * fade + mass
        for j in range(0, KVL, 128):
            acc[:, j : j + 128] = acc[:, j : j + 128] * fade + value[:, j : j + 128]

    @pl.when(mine >= 0)
    def _():
        for i in range(count):
            key_copy(i).start()
        keys[width:, :] = jnp.where(iota2((WIDE - width, ctx), 1) < lengths_ref[mine], 0.0, HIDDEN).astype(BF16)

        def cached(i, depth):
            return keys[:depth, pl.ds(pl.multiple_of(i * CHUNK, CHUNK), CHUNK)]

        score(head_ref[:, :NEW_PAD], raw_odd, NEW_PAD, None, top_odd)
        score(head_ref[:, NEW_PAD:], raw_even, CHUNK, top_odd, top_even)
        weigh(head_ref[:KVL, :NEW_PAD], raw_odd, NEW_PAD, None, top_odd)
        key_copy(0).wait()

        @pl.loop(0, count // 2)
        def _(pair):
            i = pair * 2
            key_copy(i + 1).wait()
            key_copy(i + 2).wait()
            before = top_odd[...]
            score(cached(i + 1, WIDE), raw_odd, CHUNK, top_even, top_odd)
            weigh(cached(i, KVL), raw_even, CHUNK, before, top_even)
            before = top_even[...]
            score(cached(i + 2, WIDE), raw_even, CHUNK, top_odd, top_even)
            weigh(cached(i + 1, KVL), raw_odd, CHUNK, before, top_odd)

        weigh(keys[:KVL, ctx - CHUNK :], raw_even, CHUNK, top_odd[...], top_even)
        inverse = 1.0 / jnp.sum(total[...], axis=1, keepdims=True)
        answer[...] = (acc[...] * inverse).astype(BF16)
        copy = pltpu.make_async_copy(answer, out_ref, sem)
        copy.start()
        copy.wait()


def collect_kernel(strags, toks, heads, owners_ref, got_ref, out_ref, held):
    per = toks * heads
    for s in range(strags):
        held[s * per : (s + 1) * per, :] = got_ref[owners_ref[s]]
    shape = (toks * strags, strags * per)
    row, col = iota2(shape, 0), iota2(shape, 1)
    for h in range(heads):
        pick = (col == row % strags * per + row // strags * heads + h).astype(F32).astype(BF16)
        lined = jnp.dot(pick, held[...], preferred_element_type=F32).astype(BF16)
        for t in range(toks):
            out_ref[t, :, h * KVL : (h + 1) * KVL] = lined[t * strags : (t + 1) * strags]


def shards(cache, lengths, owners, positions, q_nope, q_rope, absorb_weight, new_latent):
    ranks = lax.axis_size("seq")
    me = lax.axis_index("seq").astype(jnp.int32).reshape(1)
    strags, toks = positions.shape
    heads = absorb_weight.shape[0]
    per = toks * heads
    ctx, width = cache.shape[1:]
    rows = ranks * per
    smem = pl.BlockSpec(memory_space=pltpu.SMEM)
    vmem = pl.BlockSpec(memory_space=pltpu.VMEM)
    anyspace = pl.BlockSpec(memory_space=pl.ANY)
    sending = pl.pallas_call(
        functools.partial(absorb_kernel, strags, toks, heads),
        out_shape=jax.ShapeDtypeStruct((ranks, per, WIDE), BF16),
        in_specs=[smem, anyspace, anyspace, anyspace],
        out_specs=anyspace,
        scratch_shapes=[
            VMEM((toks, strags, heads * NOPE), BF16),
            VMEM((toks, strags, heads * ROPE), BF16),
            VMEM((heads * NOPE, KVL), BF16),
            VMEM((toks * strags, heads * NOPE), F32),
            VMEM((toks * strags, heads * ROPE), F32),
            VMEM((strags * per, WIDE), BF16),
            pltpu.SemaphoreType.DMA((3,)),
            pltpu.SemaphoreType.DMA((strags,)),
        ],
        compiler_params=pltpu.CompilerParams(vmem_limit_bytes=60 * 2**20),
        name="absorb",
    )(
        owners,
        jnp.transpose(q_nope, (1, 0, 2)),
        jnp.transpose(q_rope, (1, 0, 2)),
        absorb_weight.reshape(heads * NOPE, KVL),
    )
    query = lax.all_to_all(sending, "seq", split_axis=0, concat_axis=0, tiled=True).reshape(rows, WIDE)
    seen = positions[:, None, :] <= positions[:, :, None]
    hidden = jnp.where(seen, 0.0, HIDDEN).astype(BF16)
    fresh = jnp.concatenate([jnp.transpose(new_latent, (0, 2, 1)), hidden], axis=1)
    fresh = jnp.pad(fresh, ((0, 0), (0, WIDE - width - toks), (0, 0)))
    unused = jnp.where(jnp.arange(WIDE) < width, 0.0, HIDDEN).astype(BF16)
    unused = jnp.broadcast_to(unused[None, :, None], (strags, WIDE, NEW_PAD - toks))
    fresh = jnp.concatenate([fresh, unused], axis=2)
    keys = jnp.transpose(cache[0])
    staged = pl.pallas_call(
        functools.partial(stage_kernel, strags),
        out_shape=jax.ShapeDtypeStruct((WIDE, HEAD), BF16),
        in_specs=[smem, smem, smem, anyspace, anyspace],
        out_specs=anyspace,
        scratch_shapes=[VMEM((WIDE - width, HEAD - NEW_PAD), BF16), pltpu.SemaphoreType.DMA((3,))],
        compiler_params=pltpu.CompilerParams(vmem_limit_bytes=24 * 2**20),
        cost_estimate=pl.CostEstimate(flops=0, bytes_accessed=4 * WIDE * HEAD, transcendentals=0),
        name="stage",
    )(me, owners, lengths, fresh, keys)
    answer = pl.pallas_call(
        functools.partial(attend_kernel, strags),
        out_shape=jax.ShapeDtypeStruct((rows, KVL), BF16),
        in_specs=[smem, smem, smem, vmem, vmem, anyspace],
        out_specs=anyspace,
        scratch_shapes=[
            VMEM((WIDE, ctx), BF16),
            VMEM((rows, CHUNK), F32),
            VMEM((rows, CHUNK), F32),
            VMEM((rows, KVL), F32),
            VMEM((rows, 128), F32),
            VMEM((rows, 128), F32),
            VMEM((rows, 128), F32),
            VMEM((rows, KVL), BF16),
            pltpu.SemaphoreType.DMA((ctx // CHUNK,)),
            pltpu.SemaphoreType.DMA,
        ],
        compiler_params=pltpu.CompilerParams(vmem_limit_bytes=48 * 2**20),
        name="attend",
    )(me, owners, lengths, query, staged, keys)
    got = lax.all_to_all(answer.reshape(ranks, per, KVL), "seq", split_axis=0, concat_axis=0, tiled=True)
    out = pl.pallas_call(
        functools.partial(collect_kernel, strags, toks, heads),
        out_shape=jax.ShapeDtypeStruct((toks, strags, heads * KVL), BF16),
        in_specs=[smem, vmem],
        out_specs=vmem,
        scratch_shapes=[VMEM((strags * per, KVL), BF16)],
        compiler_params=pltpu.CompilerParams(vmem_limit_bytes=32 * 2**20),
        name="collect",
    )(owners, got)
    return jnp.transpose(out, (1, 0, 2))


def solution(mesh):
    in_specs = (
        P(("grp", "seq"), None, None),
        P("grp"),
        P("grp"),
        P("grp", None),
        P("grp", None, "seq"),
        P("grp", None, "seq"),
        P("seq", None, None),
        P("grp", None, None),
    )
    out_specs = P("grp", None, "seq")
    return jax.shard_map(shards, mesh=mesh, in_specs=in_specs, out_specs=out_specs, check_vma=False)
```

time: 311 us -> 59.6 us (0.19)
  waiting for transfers between devices: 125 us -> 12.5 us
  blocking collectives: 125 us -> 27.2 us
  local copies, waits for them, and re-layouts: 22.9 us -> 2.87 us
  between operations: 13.6 us -> 0.1 us
  matrix products: 8.19 us -> 0 us
  Pallas kernels: 0 us -> 5.54 us
    psum x1 -> x0, blocking collectives: 65.1 us -> none  [shards(): total = lax.psum(local_total, 'seq')]
    pmax x1 -> x0, blocking collectives: 60.4 us -> none  [shards(): row_top = lax.pmax(local_top, 'seq')]
    all_to_all x1, waiting for transfers between devices: 61 us -> 12.5 us  [shards(): lax.all_to_all(sending, 'seq', split_axis=0, concat_axis=0, tiled=True)]
    reduce_scatter x1 -> x0, waiting for transfers between devices: 40.1 us -> none  [shards(): lax.psum_scatter(partial_value.astype(jnp.bfloat16), 'seq', scatter_dimen...]
    all_to_all x0 -> x1, blocking collectives: none -> 27.2 us  [shards(): lax.all_to_all(answer.reshape(ranks, per, KVL), 'seq', split_axis=0, conc...]
    all_gather x1 -> x0, waiting for transfers between devices: 23.7 us -> none  [shards(): query = lax.all_gather(local_query, 'seq', axis=2, tiled=True)]
    reshape x5 -> x0, local copies, waits for them, and re-layouts: 8.39 us -> none  [the longest x1 6.57 us: shards(): sending = cache.reshape(piece_count, piece_rows, latent_width)]
    dot_general x5 -> x0, matrix products: 8.19 us -> none  [the longest x1 2.8 us: shards(): jnp.einsum('sqk,skc->sqc', new_weights.astype(jnp.bfloat16), new_latent[:...]
  transfers between devices with their start and end apart: 3 -> 1, of which waited for: 3 -> 1; matrix products, arithmetic and copies ran while one was open for 4% -> 2% of each run, Pallas kernels for 0% -> 1%
where the time goes in v1:
time: 59.6 us; the launch traced here: 59.2 us
  blocking collectives  27.2 us (46%)
  waiting for transfers between devices  12.5 us (21%)
  starting transfers between devices  10.5 us (18%)
  Pallas kernels  5.54 us (9%)
  local copies, waits for them, and re-layouts  2.87 us (5%)
    all_to_all x1, blocking collectives, shards(): lax.all_to_all(answer.reshape(ranks, per, KVL), 'seq', split_axis=0, conc...  27.2 us
    all_to_all x1, waiting for transfers between devices, shards(): lax.all_to_all(sending, 'seq', split_axis=0, concat_axis=0, tiled=True)  12.5 us
    all_to_all x1, starting transfers between devices, shards(): lax.all_to_all(sending, 'seq', split_axis=0, concat_axis=0, tiled=True)  10.5 us
    pallas_call x1, Pallas kernels, shards(): pl.pallas_call(functools.partial(absorb_kernel, strags, toks, heads), out...  2.86 us
    unnamed x11, local copies, waits for them, and re-layouts  2.36 us
    pallas_call x1, Pallas kernels, shards(): pl.pallas_call(functools.partial(collect_kernel, strags, toks, heads), ou...  1.48 us
  transfers between devices with their start and end apart: 1, of which 1 were waited for; matrix products, arithmetic and copies ran while one was open for 2% of the time, Pallas kernels for 1%

profile of v1, /device:TPU:1, one launch (start us, length us, event | category | flops | bytes accessed | tf_op | source)
XLA Modules:
  0.0 59.2 jit_solution(16064302238747870510)
XLA Ops:
  0.0 2.9 %absorb.1 = bf16[16,48,640]{2,1,0:T(8,128)(2,1)} custom-call(s32[4]{0:T(128)} %owners_ref.7, bf16[12,4,512]{2,1,0:T(4,128)(2,1)} %bitcast.17, bf16[12,4,256]{2,1,0:T(4,128)(2,1)} %bitcast.18, bf16[512,512]{1,0:T(8,128)(2,1)} %bitcast.15), custom_call_target="tpu_custom_call" | custom-call | tf_op jit(solution)/shard_map/absorb/pallas_call | solution.py:193
  2.9 0.0 copy-start.4
  2.9 0.0 copy-start.3
  2.9 10.5 %all-to-all-start = ((bf16[16,48,640]{2,1,0:T(8,128)(2,1)}), bf16[16,48,640]{2,1,0:T(8,128)(2,1)S(1)}, u32[]{:S(2)}, u32[]{:S(2)}) async-start(bf16[16,48,640]{2,1,0:T(8,128)(2,1)} %absorb.1), calls=%async_computation | async-start | bytes 1966080 | tf_op jit(solution)/shard_map/all_to_all | solution.py:216
  13.3 0.0 copy-done.4
  13.3 0.1 copy.10
  13.4 0.1 select_convert_fusion
  13.5 0.0 copy-done.3
  13.5 0.1 pad_maximum_fusion
  13.6 0.4 copy.11
  14.0 0.0 copy-start.1
  14.0 0.0 copy-start.2
  14.0 0.2 broadcast_in_dim.28
  14.2 0.4 fusion.1.new_ref
  14.6 0.1 copy-done.1
  14.6 0.0 copy-done.2
  14.7 0.0 copy-start
  14.7 2.2 %copy-done = bf16[1,3584,576]{1,2,0:T(8,128)(2,1)S(1)} copy-done((bf16[1,3584,576]{1,2,0:T(8,128)(2,1)S(1)}, bf16[1,3584,576]{1,2,0:T(8,128)(2,1)}, u32[]{:S(2)}) %copy-start) | copy-done | bytes 4128792
  16.8 0.6 stage.1.head_ref
  17.4 12.5 %all-to-all-done = bf16[16,48,640]{2,1,0:T(8,128)(2,1)S(1)} async-done(((bf16[16,48,640]{2,1,0:T(8,128)(2,1)}), bf16[16,48,640]{2,1,0:T(8,128)(2,1)S(1)}, u32[]{:S(2)}, u32[]{:S(2)}) %all-to-all-start) | async-done | bytes 983072 | tf_op jit(solution)/shard_map/all_to_all | solution.py:216
  29.9 0.6 %attend.1 = bf16[768,512]{1,0:T(8,128)(2,1)S(1)} custom-call(s32[1]{0:T(128)} %bitcast.me_ref, s32[4]{0:T(128)S(1)} %copy-done.1, s32[4]{0:T(128)S(1)} %copy-done.2, bf16[768,640]{1,0:T(8,128)(2,1)S(1)} %bitcast.13, bf16[640,640]{1,0:T(8,128)(2,1)S(1)} %stage.1.head_ref, bf16[576,3584]{1,0:T(8,128)(2,1)} %bitcast.11), custom_call_target="tpu_custom_call" | custom-call | tf_op jit(solution)/shard_map/attend/pallas_call | solution.py:235
  30.6 27.2 %all_to_all.10.got_ref = bf16[16,48,512]{2,1,0:T(8,128)(2,1)S(1)} all-to-all(bf16[16,48,512]{2,1,0:T(8,128)(2,1)S(1)} %bitcast.14), channel_id=1, replica_groups=mesh['grp'=32,'seq'=16] {'seq'}, dimensions={0} | all-to-all | bytes 1572864 | tf_op jit(solution)/shard_map/all_to_all | solution.py:255
  57.8 1.5 %collect.1 = bf16[12,4,2048]{2,1,0:T(4,128)(2,1)} custom-call(s32[4]{0:T(128)S(1)} %copy-done.1, bf16[16,48,512]{2,1,0:T(8,128)(2,1)S(1)} %all_to_all.10.got_ref), custom_call_target="tpu_custom_call" | custom-call | tf_op jit(solution)/shard_map/collect/pallas_call | solution.py:256
  (1 shorter events, 0.0 us)
Async XLA Ops:
  2.9 10.5 %copy-start.4 = (s32[4,12]{1,0:T(4,128)S(1)}, s32[4,12]{1,0:T(4,128)}, u32[]{:S(2)}) copy-start(s32[4,12]{1,0:T(4,128)} %param.11) | copy-start | bytes 580
  2.9 10.7 %copy-start.3 = (bf16[4,12,576]{2,0,1:T(4,128)(2,1)S(1)}, bf16[4,12,576]{2,0,1:T(4,128)(2,1)}, u32[]{:S(2)}) copy-start(bf16[4,12,576]{2,0,1:T(4,128)(2,1)} %param.15) | copy-start | bytes 165892
  2.9 27.0 %all-to-all-start = ((bf16[16,48,640]{2,1,0:T(8,128)(2,1)}), bf16[16,48,640]{2,1,0:T(8,128)(2,1)S(1)}, u32[]{:S(2)}, u32[]{:S(2)}) async-start(bf16[16,48,640]{2,1,0:T(8,128)(2,1)} %absorb.1), calls=%async_computation | async-start | bytes 1966080 | tf_op jit(solution)/shard_map/all_to_all | solution.py:216
  14.0 0.7 %copy-start.1 = (s32[4]{0:T(128)S(1)}, s32[4]{0:T(128)}, u32[]{:S(2)}) copy-start(s32[4]{0:T(128)} %owners_ref.7) | copy-start | bytes 52
  14.0 0.7 %copy-start.2 = (s32[4]{0:T(128)S(1)}, s32[4]{0:T(128)}, u32[]{:S(2)}) copy-start(s32[4]{0:T(128)} %lengths_ref.3) | copy-start | bytes 52
  14.7 2.2 %copy-start = (bf16[1,3584,576]{1,2,0:T(8,128)(2,1)S(1)}, bf16[1,3584,576]{1,2,0:T(8,128)(2,1)}, u32[]{:S(2)}) copy-start(bf16[1,3584,576]{1,2,0:T(8,128)(2,1)} %param.8) | copy-start | bytes 12386308

commit v2 on v1

--- a/solution.py
+++ b/solution.py
@@ -13,7 +13,7 @@
 NOPE = 128
 NEW_PAD = 128
 CHUNK = 512
-HEAD = NEW_PAD + CHUNK
+HEAD = NEW_PAD + CHUNK // 2
 F32 = jnp.float32
 BF16 = jnp.bfloat16
 HIDDEN = -1e30
@@ -32,29 +32,39 @@
     ]
     for copy in copies:
         copy.start()
-    rows = strags * toks * heads
     per = toks * heads
-    wide = (rows, toks * strags)
-    row, col = iota2(wide, 0), iota2(wide, 1)
-    pick = (col == (row % per) // heads * strags + row // per).astype(F32).astype(BF16)
-    fold = (iota2((heads * ROPE, ROPE), 0) % ROPE == iota2((heads * ROPE, ROPE), 1)).astype(F32).astype(BF16)
-    tail = (rows, WIDE - KVL - ROPE)
-    marks = (iota2(tail, 1) == iota2(tail, 0) % per // heads).astype(F32).astype(BF16)
+    rows = strags * per
+
+    def parts_of(shape):
+        row = iota2(shape, 0)
+        strag = sum((row >= s * per).astype(jnp.int32) for s in range(1, strags))
+        line = row - strag * per
+        return strag, line // heads, line & (heads - 1)
+
+    shape = (rows, toks * strags)
+    strag, tok, _ = parts_of(shape)
+    pick = (iota2(shape, 1) == tok * strags + strag).astype(F32).astype(BF16)
+    shape = (heads * ROPE, ROPE)
+    fold = ((iota2(shape, 0) & (ROPE - 1)) == iota2(shape, 1)).astype(F32).astype(BF16)
+    shape = (rows, WIDE - KVL - ROPE)
+    marks = (iota2(shape, 1) == parts_of(shape)[1]).astype(F32).astype(BF16)
+    _, _, head = parts_of((rows, 1))
 
     def spread(ref, width):
         copied = jnp.dot(pick, ref[...].astype(BF16), preferred_element_type=F32)
-        shape = (rows, heads * width)
-        own = iota2(shape, 1) // width == iota2(shape, 0) % heads
-        return jnp.where(own, copied, 0.0).astype(BF16)
+        pieces = []
+        for h in range(heads):
+            pieces.append(jnp.where(head == h, copied[:, h * width : (h + 1) * width], 0.0))
+        return pieces
 
     copies[0].wait()
     copies[1].wait()
     for t in range(toks):
         nope_rows[t * strags : (t + 1) * strags, :] = nope_ref[t].astype(F32)
         rope_rows[t * strags : (t + 1) * strags, :] = rope_ref[t].astype(F32)
-    roped = jnp.dot(spread(rope_rows, ROPE), fold, preferred_element_type=F32).astype(BF16)
+    expanded = jnp.concatenate(spread(nope_rows, NOPE), axis=1).astype(BF16)
+    roped = sum(spread(rope_rows, ROPE)).astype(BF16)
     slots[:, KVL:] = jnp.concatenate([roped, marks], axis=1)
-    expanded = spread(nope_rows, NOPE)
     copies[2].wait()
     slots[:, :KVL] = jnp.dot(expanded, weight_ref[...], preferred_element_type=F32).astype(BF16)
     leaving = [
@@ -66,16 +76,17 @@
         copy.wait()
 
 
-def straggler_here(strags, me_ref, owners_ref):
+def straggler_here(strags, info_ref):
     mine = jnp.int32(-1)
     for s in range(strags):
-        mine = jnp.where(owners_ref[s] == me_ref[0], s, mine)
+        mine = jnp.where(info_ref[1 + s] == info_ref[0], s, mine)
     return mine
 
 
-def stage_kernel(strags, me_ref, owners_ref, lengths_ref, new_ref, keys_ref, out_ref, tail, sems):
-    mine = straggler_here(strags, me_ref, owners_ref)
+def stage_kernel(strags, info_ref, new_ref, keys_ref, out_ref, tail_ref, hidden, sems):
+    mine = straggler_here(strags, info_ref)
     width = keys_ref.shape[0]
+    spare = WIDE - width
     count = out_ref.shape[1] - NEW_PAD
 
     @pl.when(mine >= 0)
@@ -85,25 +96,35 @@
                 keys_ref.at[:, pl.ds(0, count)], out_ref.at[pl.ds(0, width), pl.ds(NEW_PAD, count)], sems.at[0]
             ),
             pltpu.make_async_copy(new_ref.at[mine], out_ref.at[:, pl.ds(0, NEW_PAD)], sems.at[1]),
-            pltpu.make_async_copy(tail, out_ref.at[pl.ds(width, WIDE - width), pl.ds(NEW_PAD, count)], sems.at[2]),
+            pltpu.make_async_copy(
+                hidden.at[:, pl.ds(0, count)], out_ref.at[pl.ds(width, spare), pl.ds(NEW_PAD, count)], sems.at[2]
+            ),
+            pltpu.make_async_copy(hidden.at[:, pl.ds(count, tail_ref.shape[1])], tail_ref, sems.at[3]),
         ]
         copies[0].start()
         copies[1].start()
-        tail[...] = jnp.where(iota2(tail.shape, 1) < lengths_ref[mine], 0.0, HIDDEN).astype(BF16)
+        length = info_ref[1 + strags + mine]
+        hidden[...] = jnp.where(iota2(hidden.shape, 1) < length, 0.0, HIDDEN).astype(BF16)
         copies[2].start()
+        copies[3].start()
         for copy in copies:
             copy.wait()
 
 
-def attend_kernel(strags, me_ref, owners_ref, lengths_ref, query_ref, head_ref, keys_ref, out_ref, keys, raw_even, raw_odd, acc, total, top_even, top_odd, answer, key_sems, sem):
-    mine = straggler_here(strags, me_ref, owners_ref)
+def attend_kernel(strags, info_ref, query_ref, head_ref, tail_ref, keys_ref, out_ref, keys, raw_even, raw_odd, acc, total, top_even, top_odd, key_sems, tail_sem):
+    mine = straggler_here(strags, info_ref)
     width, ctx = keys_ref.shape
-    count = ctx // CHUNK
+    first = head_ref.shape[1] - NEW_PAD
+    count = (ctx - first) // CHUNK
+    last = ctx - first - count * CHUNK
     factor = math.log2(math.e) / math.sqrt(NOPE + ROPE)
 
-    def key_copy(i):
-        part = pl.ds(pl.multiple_of(i * CHUNK, CHUNK), CHUNK)
-        return pltpu.make_async_copy(keys_ref.at[:, part], keys.at[pl.ds(0, width), part], key_sems.at[i])
+    def key_copy(i, size=CHUNK):
+        return pltpu.make_async_copy(
+            keys_ref.at[:, pl.ds(pl.multiple_of(first + i * CHUNK, 128), size)],
+            keys.at[pl.ds(0, width), pl.ds(pl.multiple_of(i * CHUNK, 128), size)],
+            key_sems.at[i],
+        )
 
     def score(keys_part, raw, size, top_before, top_after):
         part = jnp.dot(query_ref[...], keys_part, preferred_element_type=F32)
@@ -134,42 +155,53 @@
 
     @pl.when(mine >= 0)
     def _():
+        masks = pltpu.make_async_copy(tail_ref, keys.at[pl.ds(width, WIDE - width)], tail_sem)
+        masks.start()
         for i in range(count):
             key_copy(i).start()
-        keys[width:, :] = jnp.where(iota2((WIDE - width, ctx), 1) < lengths_ref[mine], 0.0, HIDDEN).astype(BF16)
-
-        def cached(i, depth):
-            return keys[:depth, pl.ds(pl.multiple_of(i * CHUNK, CHUNK), CHUNK)]
+        key_copy(count, last).start()
+
+        def cached(i, depth, size=CHUNK):
+            return keys[:depth, pl.ds(pl.multiple_of(i * CHUNK, 128), size)]
 
         score(head_ref[:, :NEW_PAD], raw_odd, NEW_PAD, None, top_odd)
-        score(head_ref[:, NEW_PAD:], raw_even, CHUNK, top_odd, top_even)
+        score(head_ref[:, NEW_PAD:], raw_even, first, top_odd, top_even)
         weigh(head_ref[:KVL, :NEW_PAD], raw_odd, NEW_PAD, None, top_odd)
+        masks.wait()
         key_copy(0).wait()
-
-        @pl.loop(0, count // 2)
+        before = top_odd[...]
+        score(cached(0, WIDE), raw_odd, CHUNK, top_even, top_odd)
+        weigh(head_ref[:KVL, NEW_PAD:], raw_even, first, before, top_even)
+
+        @pl.loop(0, count // 2 - 1)
         def _(pair):
             i = pair * 2
             key_copy(i + 1).wait()
             key_copy(i + 2).wait()
+            before = top_even[...]
+            score(cached(i + 1, WIDE), raw_even, CHUNK, top_odd, top_even)
+            weigh(cached(i, KVL), raw_odd, CHUNK, before, top_odd)
             before = top_odd[...]
-            score(cached(i + 1, WIDE), raw_odd, CHUNK, top_even, top_odd)
-            weigh(cached(i, KVL), raw_even, CHUNK, before, top_even)
-            before = top_even[...]
-            score(cached(i + 2, WIDE), raw_even, CHUNK, top_odd, top_even)
-            weigh(cached(i + 1, KVL), raw_odd, CHUNK, before, top_odd)
-
-        weigh(keys[:KVL, ctx - CHUNK :], raw_even, CHUNK, top_odd[...], top_even)
+            score(cached(i + 2, WIDE), raw_odd, CHUNK, top_even, top_odd)
+            weigh(cached(i + 1, KVL), raw_even, CHUNK, before, top_even)
+
+        key_copy(count - 1).wait()
+        key_copy(count, last).wait()
+        before = top_even[...]
+        score(cached(count - 1, WIDE), raw_even, CHUNK, top_odd, top_even)
+        weigh(cached(count - 2, KVL), raw_odd, CHUNK, before, top_odd)
+        before = top_odd[...]
+        score(cached(count, WIDE, last), raw_odd, last, top_even, top_odd)
+        weigh(cached(count - 1, KVL), raw_even, CHUNK, before, top_even)
+        weigh(cached(count, KVL, last), raw_odd, last, top_even[...], top_odd)
         inverse = 1.0 / jnp.sum(total[...], axis=1, keepdims=True)
-        answer[...] = (acc[...] * inverse).astype(BF16)
-        copy = pltpu.make_async_copy(answer, out_ref, sem)
-        copy.start()
-        copy.wait()
-
-
-def collect_kernel(strags, toks, heads, owners_ref, got_ref, out_ref, held):
+        out_ref[...] = (acc[...] * inverse).astype(BF16)
+
+
+def collect_kernel(strags, toks, heads, starts_ref, got_ref, out_ref, held):
     per = toks * heads
     for s in range(strags):
-        held[s * per : (s + 1) * per, :] = got_ref[owners_ref[s]]
+        held[s * per : (s + 1) * per, :] = got_ref[pl.ds(pl.multiple_of(starts_ref[s], 16), per), :]
     shape = (toks * strags, strags * per)
     row, col = iota2(shape, 0), iota2(shape, 1)
     for h in range(heads):
@@ -222,36 +254,37 @@
     unused = jnp.broadcast_to(unused[None, :, None], (strags, WIDE, NEW_PAD - toks))
     fresh = jnp.concatenate([fresh, unused], axis=2)
     keys = jnp.transpose(cache[0])
-    staged = pl.pallas_call(
+    info = jnp.concatenate([me, owners, lengths])
+    late = ctx - (HEAD - NEW_PAD)
+    staged, masks = pl.pallas_call(
         functools.partial(stage_kernel, strags),
-        out_shape=jax.ShapeDtypeStruct((WIDE, HEAD), BF16),
-        in_specs=[smem, smem, smem, anyspace, anyspace],
-        out_specs=anyspace,
-        scratch_shapes=[VMEM((WIDE - width, HEAD - NEW_PAD), BF16), pltpu.SemaphoreType.DMA((3,))],
+        out_shape=[jax.ShapeDtypeStruct((WIDE, HEAD), BF16), jax.ShapeDtypeStruct((WIDE - width, late), BF16)],
+        in_specs=[smem, anyspace, anyspace],
+        out_specs=[anyspace, anyspace],
+        scratch_shapes=[VMEM((WIDE - width, ctx), BF16), pltpu.SemaphoreType.DMA((4,))],
         compiler_params=pltpu.CompilerParams(vmem_limit_bytes=24 * 2**20),
         cost_estimate=pl.CostEstimate(flops=0, bytes_accessed=4 * WIDE * HEAD, transcendentals=0),
         name="stage",
-    )(me, owners, lengths, fresh, keys)
+    )(info, fresh, keys)
     answer = pl.pallas_call(
         functools.partial(attend_kernel, strags),
         out_shape=jax.ShapeDtypeStruct((rows, KVL), BF16),
-        in_specs=[smem, smem, smem, vmem, vmem, anyspace],
-        out_specs=anyspace,
+        in_specs=[smem, vmem, vmem, anyspace, anyspace],
+        out_specs=vmem,
         scratch_shapes=[
-            VMEM((WIDE, ctx), BF16),
+            VMEM((WIDE, late), BF16),
             VMEM((rows, CHUNK), F32),
             VMEM((rows, CHUNK), F32),
             VMEM((rows, KVL), F32),
             VMEM((rows, 128), F32),
             VMEM((rows, 128), F32),
             VMEM((rows, 128), F32),
-            VMEM((rows, KVL), BF16),
-            pltpu.SemaphoreType.DMA((ctx // CHUNK,)),
+            pltpu.SemaphoreType.DMA((late // CHUNK + 1,)),
             pltpu.SemaphoreType.DMA,
         ],
         compiler_params=pltpu.CompilerParams(vmem_limit_bytes=48 * 2**20),
         name="attend",
-    )(me, owners, lengths, query, staged, keys)
+    )(info, query, staged, masks, keys)
     got = lax.all_to_all(answer.reshape(ranks, per, KVL), "seq", split_axis=0, concat_axis=0, tiled=True)
     out = pl.pallas_call(
         functools.partial(collect_kernel, strags, toks, heads),
@@ -261,7 +294,7 @@
         scratch_shapes=[VMEM((strags * per, KVL), BF16)],
         compiler_params=pltpu.CompilerParams(vmem_limit_bytes=32 * 2**20),
         name="collect",
-    )(owners, got)
+    )(owners * per, got.reshape(rows, KVL))
     return jnp.transpose(out, (1, 0, 2))
 
 

time: 59.6 us -> 60.5 us (1.015)
  blocking collectives: 27.2 us -> 0 us
  waiting for transfers between devices: 12.5 us -> 26.9 us
  starting transfers between devices: 10.5 us -> 23.3 us
  Pallas kernels: 5.54 us -> 6.38 us
    all_to_all x1 -> x0, blocking collectives: 27.2 us -> none  [shards(): lax.all_to_all(answer.reshape(ranks, per, KVL), 'seq', split_axis=0, conc...]
    all_to_all x0 -> x1, waiting for transfers between devices: none -> 14.4 us  [shards(): lax.all_to_all(answer.reshape(ranks, per, KVL), 'seq', split_axis=0, conc...]
    all_to_all x0 -> x1, starting transfers between devices: none -> 12.8 us  [shards(): lax.all_to_all(answer.reshape(ranks, per, KVL), 'seq', split_axis=0, conc...]
    pallas_call x1, Pallas kernels: 0.63 us -> 1.5 us  [shards(): pl.pallas_call(functools.partial(attend_kernel, strags), out_shape=jax.Sh...]
  transfers between devices with their start and end apart: 1 -> 2, of which waited for: 1 -> 2; matrix products, arithmetic and copies ran while one was open for 2% -> 2% of each run, Pallas kernels for 1% -> 1%
where the time goes in v2:
time: 60.5 us; the launch traced here: 60.1 us
  waiting for transfers between devices  26.9 us (44%)
  starting transfers between devices  23.3 us (39%)
  Pallas kernels  6.38 us (11%)
  local copies, waits for them, and re-layouts  2.8 us (5%)
  other arithmetic  0.65 us (1%)
    all_to_all x1, waiting for transfers between devices, shards(): lax.all_to_all(answer.reshape(ranks, per, KVL), 'seq', split_axis=0, conc...  14.4 us
    all_to_all x1, starting transfers between devices, shards(): lax.all_to_all(answer.reshape(ranks, per, KVL), 'seq', split_axis=0, conc...  12.8 us
    all_to_all x1, waiting for transfers between devices, shards(): lax.all_to_all(sending, 'seq', split_axis=0, concat_axis=0, tiled=True)  12.5 us
    all_to_all x1, starting transfers between devices, shards(): lax.all_to_all(sending, 'seq', split_axis=0, concat_axis=0, tiled=True)  10.5 us
    pallas_call x1, Pallas kernels, shards(): pl.pallas_call(functools.partial(absorb_kernel, strags, toks, heads), out...  2.81 us
    unnamed x11, local copies, waits for them, and re-layouts  2.28 us
    pallas_call x1, Pallas kernels, shards(): pl.pallas_call(functools.partial(attend_kernel, strags), out_shape=jax.Sh...  1.5 us
    pallas_call x1, Pallas kernels, shards(): pl.pallas_call(functools.partial(collect_kernel, strags, toks, heads), ou...  1.48 us
  transfers between devices with their start and end apart: 2, of which 2 were waited for; matrix products, arithmetic and copies ran while one was open for 2% of the time, Pallas kernels for 1%

profile of v2, /device:TPU:1, one launch (start us, length us, event | category | flops | bytes accessed | tf_op | source)
XLA Modules:
  0.0 60.1 jit_solution(17694709936180896547)
XLA Ops:
  0.0 2.8 %absorb.1 = bf16[16,48,640]{2,1,0:T(8,128)(2,1)} custom-call(s32[4]{0:T(128)} %owners_ref.1, bf16[12,4,512]{2,1,0:T(4,128)(2,1)} %bitcast.18, bf16[12,4,256]{2,1,0:T(4,128)(2,1)} %bitcast.19, bf16[512,512]{1,0:T(8,128)(2,1)} %bitcast.16), custom_call_target="tpu_custom_call" | custom-call | tf_op jit(solution)/shard_map/absorb/pallas_call | solution.py:225
  2.8 0.0 copy-start.2
  2.8 0.0 copy-start.1
  2.8 0.0 copy-start.3
  2.9 0.0 copy-start.4
  2.9 10.5 %all-to-all-start = ((bf16[16,48,640]{2,1,0:T(8,128)(2,1)}), bf16[16,48,640]{2,1,0:T(8,128)(2,1)S(1)}, u32[]{:S(2)}, u32[]{:S(2)}) async-start(bf16[16,48,640]{2,1,0:T(8,128)(2,1)} %absorb.1), calls=%async_computation | async-start | bytes 1966080 | tf_op jit(solution)/shard_map/all_to_all | solution.py:248
  13.3 0.0 copy-done.2
  13.3 0.1 copy.10
  13.4 0.1 select_convert_fusion
  13.5 0.0 copy-done.1
  13.5 0.1 pad_maximum_fusion
  13.6 0.4 copy.11
  14.0 0.0 copy-done.3
  14.0 0.0 copy-done.4
  14.0 0.1 pad_add_fusion.info_ref
  14.1 0.2 broadcast_in_dim.28
  14.2 0.4 fusion.1.new_ref
  14.6 0.0 copy-start
  14.6 2.2 %copy-done = bf16[1,3584,576]{1,2,0:T(8,128)(2,1)S(1)} copy-done((bf16[1,3584,576]{1,2,0:T(8,128)(2,1)S(1)}, bf16[1,3584,576]{1,2,0:T(8,128)(2,1)}, u32[]{:S(2)}) %copy-start) | copy-done | bytes 4128792
  16.8 0.6 stage.1
  17.4 12.5 %all-to-all-done = bf16[16,48,640]{2,1,0:T(8,128)(2,1)S(1)} async-done(((bf16[16,48,640]{2,1,0:T(8,128)(2,1)}), bf16[16,48,640]{2,1,0:T(8,128)(2,1)S(1)}, u32[]{:S(2)}, u32[]{:S(2)}) %all-to-all-start) | async-done | bytes 983072 | tf_op jit(solution)/shard_map/all_to_all | solution.py:248
  29.9 1.5 %attend.1 = bf16[768,512]{1,0:T(8,128)(2,1)} custom-call(s32[9]{0:T(128)S(1)} %pad_add_fusion.info_ref, bf16[768,640]{1,0:T(8,128)(2,1)S(1)} %bitcast.14, bf16[640,384]{1,0:T(8,128)(2,1)S(1)} %get-tuple-element.7.head_ref, bf16[64,3328]{1,0:T(8,128)(2,1)S(1)} %get-tuple-element.8.tail_ref, bf16[576,3584]{1,0:T(8,128)(2,1)} %bitcast.12), custom_call_target="tpu_custom_call" | custom-call | tf_op jit(solution)/shard_map/attend/pallas_call | solution.py:269
  31.4 12.8 %all-to-all-start.1 = ((bf16[16,48,512]{2,1,0:T(8,128)(2,1)}), bf16[16,48,512]{2,1,0:T(8,128)(2,1)S(1)}, u32[]{:S(2)}, u32[]{:S(2)}) async-start(bf16[16,48,512]{2,1,0:T(8,128)(2,1)} %bitcast.8), calls=%async_computation.1 | async-start | bytes 1572864 | tf_op jit(solution)/shard_map/all_to_all | solution.py:288
  44.2 14.4 %all-to-all-done.1 = bf16[16,48,512]{2,1,0:T(8,128)(2,1)S(1)} async-done(((bf16[16,48,512]{2,1,0:T(8,128)(2,1)}), bf16[16,48,512]{2,1,0:T(8,128)(2,1)S(1)}, u32[]{:S(2)}, u32[]{:S(2)}) %all-to-all-start.1) | async-done | bytes 786464 | tf_op jit(solution)/shard_map/all_to_all | solution.py:288
  58.6 1.5 %collect.1 = bf16[12,4,2048]{2,1,0:T(4,128)(2,1)} custom-call(s32[4]{0:T(128)S(1)} %broadcast_multiply_fusion.starts_ref, bf16[768,512]{1,0:T(8,128)(2,1)S(1)} %bitcast.15), custom_call_target="tpu_custom_call" | custom-call | tf_op jit(solution)/shard_map/collect/pallas_call | solution.py:289
  (2 shorter events, 0.0 us)
Async XLA Ops:
  2.8 10.5 %copy-start.2 = (s32[4,12]{1,0:T(4,128)S(1)}, s32[4,12]{1,0:T(4,128)}, u32[]{:S(2)}) copy-start(s32[4,12]{1,0:T(4,128)} %param.11) | copy-start | bytes 580
  2.8 10.7 %copy-start.1 = (bf16[4,12,576]{2,0,1:T(4,128)(2,1)S(1)}, bf16[4,12,576]{2,0,1:T(4,128)(2,1)}, u32[]{:S(2)}) copy-start(bf16[4,12,576]{2,0,1:T(4,128)(2,1)} %param.15) | copy-start | bytes 165892
  2.8 11.1 %copy-start.3 = (s32[4]{0:T(128)S(1)}, s32[4]{0:T(128)}, u32[]{:S(2)}) copy-start(s32[4]{0:T(128)} %owners_ref.1) | copy-start | bytes 52
  2.9 11.1 %copy-start.4 = (s32[4]{0:T(128)S(1)}, s32[4]{0:T(128)}, u32[]{:S(2)}) copy-start(s32[4]{0:T(128)} %param.9) | copy-start | bytes 52
  2.9 27.0 %all-to-all-start = ((bf16[16,48,640]{2,1,0:T(8,128)(2,1)}), bf16[16,48,640]{2,1,0:T(8,128)(2,1)S(1)}, u32[]{:S(2)}, u32[]{:S(2)}) async-start(bf16[16,48,640]{2,1,0:T(8,128)(2,1)} %absorb.1), calls=%async_computation | async-start | bytes 1966080 | tf_op jit(solution)/shard_map/all_to_all | solution.py:248
  14.6 2.2 %copy-start = (bf16[1,3584,576]{1,2,0:T(8,128)(2,1)S(1)}, bf16[1,3584,576]{1,2,0:T(8,128)(2,1)}, u32[]{:S(2)}) copy-start(bf16[1,3584,576]{1,2,0:T(8,128)(2,1)} %param.8) | copy-start | bytes 12386308
  31.4 27.2 %all-to-all-start.1 = ((bf16[16,48,512]{2,1,0:T(8,128)(2,1)}), bf16[16,48,512]{2,1,0:T(8,128)(2,1)S(1)}, u32[]{:S(2)}, u32[]{:S(2)}) async-start(bf16[16,48,512]{2,1,0:T(8,128)(2,1)} %bitcast.8), calls=%async_computation.1 | async-start | bytes 1572864 | tf_op jit(solution)/shard_map/all_to_all | solution.py:288

commit v3 on v2

--- a/solution.py
+++ b/solution.py
@@ -13,7 +13,7 @@
 NOPE = 128
 NEW_PAD = 128
 CHUNK = 512
-HEAD = NEW_PAD + CHUNK // 2
+HEAD = NEW_PAD + CHUNK
 F32 = jnp.float32
 BF16 = jnp.bfloat16
 HIDDEN = -1e30
@@ -99,7 +99,7 @@
             pltpu.make_async_copy(
                 hidden.at[:, pl.ds(0, count)], out_ref.at[pl.ds(width, spare), pl.ds(NEW_PAD, count)], sems.at[2]
             ),
-            pltpu.make_async_copy(hidden.at[:, pl.ds(count, tail_ref.shape[1])], tail_ref, sems.at[3]),
+            pltpu.make_async_copy(hidden, tail_ref, sems.at[3]),
         ]
         copies[0].start()
         copies[1].start()
@@ -114,44 +114,48 @@
 def attend_kernel(strags, info_ref, query_ref, head_ref, tail_ref, keys_ref, out_ref, keys, raw_even, raw_odd, acc, total, top_even, top_odd, key_sems, tail_sem):
     mine = straggler_here(strags, info_ref)
     width, ctx = keys_ref.shape
-    first = head_ref.shape[1] - NEW_PAD
-    count = (ctx - first) // CHUNK
-    last = ctx - first - count * CHUNK
+    count = ctx // CHUNK
     factor = math.log2(math.e) / math.sqrt(NOPE + ROPE)
 
-    def key_copy(i, size=CHUNK):
-        return pltpu.make_async_copy(
-            keys_ref.at[:, pl.ds(pl.multiple_of(first + i * CHUNK, 128), size)],
-            keys.at[pl.ds(0, width), pl.ds(pl.multiple_of(i * CHUNK, 128), size)],
-            key_sems.at[i],
-        )
-
-    def score(keys_part, raw, size, top_before, top_after):
+    def key_copy(i):
+        part = pl.ds(pl.multiple_of(i * CHUNK, CHUNK), CHUNK)
+        return pltpu.make_async_copy(keys_ref.at[:, part], keys.at[pl.ds(0, width), part], key_sems.at[i])
+
+    def score(keys_part, raw, top):
         part = jnp.dot(query_ref[...], keys_part, preferred_element_type=F32)
+        size = part.shape[1]
         raw[:, :size] = part
         peak = part[:, :128]
         for j in range(128, size, 128):
             peak = jnp.maximum(peak, part[:, j : j + 128])
         peak = jnp.broadcast_to(jnp.max(peak, axis=1, keepdims=True), peak.shape)
-        top_after[...] = peak if top_before is None else jnp.maximum(top_before[...], peak)
-
-    def weigh(values_part, raw, size, top_before, top_after):
-        top = top_after[...]
-        shift = top * factor
-        pieces = [jnp.exp2(raw[:, j : j + 128] * factor - shift) for j in range(0, size, 128)]
+        return peak if top is None else jnp.maximum(top, peak)
+
+    def weights(raw, size, shift):
+        return [jnp.exp2(raw[:, j : j + 128] * factor - shift) for j in range(0, size, 128)]
+
+    def gather(pieces, values_part, fade):
         mass = pieces[0]
         for piece in pieces[1:]:
             mass = mass + piece
-        weight = pieces[0] if size == 128 else jnp.concatenate(pieces, axis=1)
+        weight = pieces[0] if len(pieces) == 1 else jnp.concatenate(pieces, axis=1)
         value = lax.dot_general(weight.astype(BF16), values_part, (((1,), (1,)), ((), ())), preferred_element_type=F32)
-        if top_before is None:
+        if fade is None:
             total[...] = mass
             acc[...] = value
             return
-        fade = jnp.exp2(top_before * factor - shift)
         total[...] = total[...] * fade + mass
         for j in range(0, KVL, 128):
             acc[:, j : j + 128] = acc[:, j : j + 128] * fade + value[:, j : j + 128]
+
+    def step(keys_next, raw_next, top_next, values_now, raw_now, top_now, size_now, start):
+        top = top_now[...]
+        shift = top * factor
+        fade = None if start else jnp.exp2(top_next[...] * factor - shift)
+        pieces = weights(raw_now, size_now, shift)
+        if keys_next is not None:
+            top_next[...] = score(keys_next, raw_next, top)
+        gather(pieces, values_now, fade)
 
     @pl.when(mine >= 0)
     def _():
@@ -159,49 +163,32 @@
         masks.start()
         for i in range(count):
             key_copy(i).start()
-        key_copy(count, last).start()
-
-        def cached(i, depth, size=CHUNK):
-            return keys[:depth, pl.ds(pl.multiple_of(i * CHUNK, 128), size)]
-
-        score(head_ref[:, :NEW_PAD], raw_odd, NEW_PAD, None, top_odd)
-        score(head_ref[:, NEW_PAD:], raw_even, first, top_odd, top_even)
-        weigh(head_ref[:KVL, :NEW_PAD], raw_odd, NEW_PAD, None, top_odd)
+
+        def cached(i, depth):
+            return keys[:depth, pl.ds(pl.multiple_of(i * CHUNK, CHUNK), CHUNK)]
+
+        top_odd[...] = score(head_ref[:, :NEW_PAD], raw_odd, None)
+        step(head_ref[:, NEW_PAD:], raw_even, top_even, head_ref[:KVL, :NEW_PAD], raw_odd, top_odd, NEW_PAD, True)
         masks.wait()
         key_copy(0).wait()
-        before = top_odd[...]
-        score(cached(0, WIDE), raw_odd, CHUNK, top_even, top_odd)
-        weigh(head_ref[:KVL, NEW_PAD:], raw_even, first, before, top_even)
-
-        @pl.loop(0, count // 2 - 1)
+
+        @pl.loop(0, count // 2)
         def _(pair):
             i = pair * 2
             key_copy(i + 1).wait()
             key_copy(i + 2).wait()
-            before = top_even[...]
-            score(cached(i + 1, WIDE), raw_even, CHUNK, top_odd, top_even)
-            weigh(cached(i, KVL), raw_odd, CHUNK, before, top_odd)
-            before = top_odd[...]
-            score(cached(i + 2, WIDE), raw_odd, CHUNK, top_even, top_odd)
-            weigh(cached(i + 1, KVL), raw_even, CHUNK, before, top_even)
-
-        key_copy(count - 1).wait()
-        key_copy(count, last).wait()
-        before = top_even[...]
-        score(cached(count - 1, WIDE), raw_even, CHUNK, top_odd, top_even)
-        weigh(cached(count - 2, KVL), raw_odd, CHUNK, before, top_odd)
-        before = top_odd[...]
-        score(cached(count, WIDE, last), raw_odd, last, top_even, top_odd)
-        weigh(cached(count - 1, KVL), raw_even, CHUNK, before, top_even)
-        weigh(cached(count, KVL, last), raw_odd, last, top_even[...], top_odd)
+            step(cached(i + 1, WIDE), raw_odd, top_odd, cached(i, KVL), raw_even, top_even, CHUNK, False)
+            step(cached(i + 2, WIDE), raw_even, top_even, cached(i + 1, KVL), raw_odd, top_odd, CHUNK, False)
+
+        step(None, None, top_odd, cached(count - 1, KVL), raw_even, top_even, CHUNK, False)
         inverse = 1.0 / jnp.sum(total[...], axis=1, keepdims=True)
         out_ref[...] = (acc[...] * inverse).astype(BF16)
 
 
-def collect_kernel(strags, toks, heads, starts_ref, got_ref, out_ref, held):
+def collect_kernel(strags, toks, heads, owners_ref, got_ref, out_ref, held):
     per = toks * heads
     for s in range(strags):
-        held[s * per : (s + 1) * per, :] = got_ref[pl.ds(pl.multiple_of(starts_ref[s], 16), per), :]
+        held[s * per : (s + 1) * per, :] = got_ref[owners_ref[s]]
     shape = (toks * strags, strags * per)
     row, col = iota2(shape, 0), iota2(shape, 1)
     for h in range(heads):
@@ -255,10 +242,9 @@
     fresh = jnp.concatenate([fresh, unused], axis=2)
     keys = jnp.transpose(cache[0])
     info = jnp.concatenate([me, owners, lengths])
-    late = ctx - (HEAD - NEW_PAD)
     staged, masks = pl.pallas_call(
         functools.partial(stage_kernel, strags),
-        out_shape=[jax.ShapeDtypeStruct((WIDE, HEAD), BF16), jax.ShapeDtypeStruct((WIDE - width, late), BF16)],
+        out_shape=[jax.ShapeDtypeStruct((WIDE, HEAD), BF16), jax.ShapeDtypeStruct((WIDE - width, ctx), BF16)],
         in_specs=[smem, anyspace, anyspace],
         out_specs=[anyspace, anyspace],
         scratch_shapes=[VMEM((WIDE - width, ctx), BF16), pltpu.SemaphoreType.DMA((4,))],
@@ -272,14 +258,14 @@
         in_specs=[smem, vmem, vmem, anyspace, anyspace],
         out_specs=vmem,
         scratch_shapes=[
-            VMEM((WIDE, late), BF16),
+            VMEM((WIDE, ctx), BF16),
             VMEM((rows, CHUNK), F32),
             VMEM((rows, CHUNK), F32),
             VMEM((rows, KVL), F32),
             VMEM((rows, 128), F32),
             VMEM((rows, 128), F32),
             VMEM((rows, 128), F32),
-            pltpu.SemaphoreType.DMA((late // CHUNK + 1,)),
+            pltpu.SemaphoreType.DMA((ctx // CHUNK,)),
             pltpu.SemaphoreType.DMA,
         ],
         compiler_params=pltpu.CompilerParams(vmem_limit_bytes=48 * 2**20),
@@ -294,7 +280,7 @@
         scratch_shapes=[VMEM((strags * per, KVL), BF16)],
         compiler_params=pltpu.CompilerParams(vmem_limit_bytes=32 * 2**20),
         name="collect",
-    )(owners * per, got.reshape(rows, KVL))
+    )(owners, got)
     return jnp.transpose(out, (1, 0, 2))
 
 

time: 60.5 us -> 60.4 us (level)
  blocking collectives: 0 us -> 28 us
  waiting for transfers between devices: 26.9 us -> 12.5 us
  starting transfers between devices: 23.3 us -> 10.5 us
  Pallas kernels: 6.38 us -> 5.49 us
    all_to_all x0 -> x1, blocking collectives: none -> 28 us  [shards(): lax.all_to_all(answer.reshape(ranks, per, KVL), 'seq', split_axis=0, conc...]
    all_to_all x1 -> x0, waiting for transfers between devices: 14.4 us -> none  [shards(): lax.all_to_all(answer.reshape(ranks, per, KVL), 'seq', split_axis=0, conc...]
    all_to_all x1 -> x0, starting transfers between devices: 12.8 us -> none  [shards(): lax.all_to_all(answer.reshape(ranks, per, KVL), 'seq', split_axis=0, conc...]
    pallas_call x1, Pallas kernels: 1.5 us -> 0.62 us  [shards(): pl.pallas_call(functools.partial(attend_kernel, strags), out_shape=jax.Sh...]
  transfers between devices with their start and end apart: 2 -> 1, of which waited for: 2 -> 1; matrix products, arithmetic and copies ran while one was open for 2% -> 2% of each run, Pallas kernels for 1% -> 1%
where the time goes in v3:
time: 60.4 us; the launch traced here: 60 us
  blocking collectives  28 us (46%)
  waiting for transfers between devices  12.5 us (21%)
  starting transfers between devices  10.5 us (17%)
  Pallas kernels  5.49 us (9%)
  local copies, waits for them, and re-layouts  2.8 us (5%)
  other arithmetic  0.64 us (1%)
    all_to_all x1, blocking collectives, shards(): lax.all_to_all(answer.reshape(ranks, per, KVL), 'seq', split_axis=0, conc...  28 us
    all_to_all x1, waiting for transfers between devices, shards(): lax.all_to_all(sending, 'seq', split_axis=0, concat_axis=0, tiled=True)  12.5 us
    all_to_all x1, starting transfers between devices, shards(): lax.all_to_all(sending, 'seq', split_axis=0, concat_axis=0, tiled=True)  10.5 us
    pallas_call x1, Pallas kernels, shards(): pl.pallas_call(functools.partial(absorb_kernel, strags, toks, heads), out...  2.8 us
    unnamed x11, local copies, waits for them, and re-layouts  2.28 us
    pallas_call x1, Pallas kernels, shards(): pl.pallas_call(functools.partial(collect_kernel, strags, toks, heads), ou...  1.48 us
  transfers between devices with their start and end apart: 1, of which 1 were waited for; matrix products, arithmetic and copies ran while one was open for 2% of the time, Pallas kernels for 1%

profile of v3, /device:TPU:1, one launch (start us, length us, event | category | flops | bytes accessed | tf_op | source)
XLA Modules:
  0.0 60.0 jit_solution(16312539239034226458)
XLA Ops:
  0.0 2.8 %absorb.1 = bf16[16,48,640]{2,1,0:T(8,128)(2,1)} custom-call(s32[4]{0:T(128)} %owners_ref.3, bf16[12,4,512]{2,1,0:T(4,128)(2,1)} %bitcast.17, bf16[12,4,256]{2,1,0:T(4,128)(2,1)} %bitcast.18, bf16[512,512]{1,0:T(8,128)(2,1)} %bitcast.15), custom_call_target="tpu_custom_call" | custom-call | tf_op jit(solution)/shard_map/absorb/pallas_call | solution.py:212
  2.8 0.0 copy-start.3
  2.8 0.0 copy-start.2
  2.8 0.0 copy-start.1
  2.8 0.0 copy-start.4
  2.9 10.5 %all-to-all-start = ((bf16[16,48,640]{2,1,0:T(8,128)(2,1)}), bf16[16,48,640]{2,1,0:T(8,128)(2,1)S(1)}, u32[]{:S(2)}, u32[]{:S(2)}) async-start(bf16[16,48,640]{2,1,0:T(8,128)(2,1)} %absorb.1), calls=%async_computation | async-start | bytes 1966080 | tf_op jit(solution)/shard_map/all_to_all | solution.py:235
  13.3 0.0 copy-done.3
  13.3 0.1 copy.10
  13.4 0.1 select_convert_fusion
  13.5 0.0 copy-done.2
  13.5 0.1 pad_maximum_fusion
  13.6 0.4 copy.11
  13.9 0.0 copy-done.1
  14.0 0.0 copy-done.4
  14.0 0.1 pad_add_fusion.info_ref
  14.1 0.2 broadcast_in_dim.28
  14.2 0.4 fusion.1.new_ref
  14.6 0.0 copy-start
  14.6 2.2 %copy-done = bf16[1,3584,576]{1,2,0:T(8,128)(2,1)S(1)} copy-done((bf16[1,3584,576]{1,2,0:T(8,128)(2,1)S(1)}, bf16[1,3584,576]{1,2,0:T(8,128)(2,1)}, u32[]{:S(2)}) %copy-start) | copy-done | bytes 4128792
  16.8 0.6 stage.1
  17.4 12.5 %all-to-all-done = bf16[16,48,640]{2,1,0:T(8,128)(2,1)S(1)} async-done(((bf16[16,48,640]{2,1,0:T(8,128)(2,1)}), bf16[16,48,640]{2,1,0:T(8,128)(2,1)S(1)}, u32[]{:S(2)}, u32[]{:S(2)}) %all-to-all-start) | async-done | bytes 983072 | tf_op jit(solution)/shard_map/all_to_all | solution.py:235
  29.9 0.6 %attend.1 = bf16[768,512]{1,0:T(8,128)(2,1)S(1)} custom-call(s32[9]{0:T(128)S(1)} %pad_add_fusion.info_ref, bf16[768,640]{1,0:T(8,128)(2,1)S(1)} %bitcast.13, bf16[640,640]{1,0:T(8,128)(2,1)S(1)} %get-tuple-element.7.head_ref, bf16[64,3584]{1,0:T(8,128)(2,1)S(1)} %get-tuple-element.8.tail_ref, bf16[576,3584]{1,0:T(8,128)(2,1)} %bitcast.11), custom_call_target="tpu_custom_call" | custom-call | tf_op jit(solution)/shard_map/attend/pallas_call | solution.py:255
  30.5 28.0 %all_to_all.10.got_ref = bf16[16,48,512]{2,1,0:T(8,128)(2,1)S(1)} all-to-all(bf16[16,48,512]{2,1,0:T(8,128)(2,1)S(1)} %bitcast.14), channel_id=1, replica_groups=mesh['grp'=32,'seq'=16] {'seq'}, dimensions={0} | all-to-all | bytes 1572864 | tf_op jit(solution)/shard_map/all_to_all | solution.py:274
  58.6 1.5 %collect.1 = bf16[12,4,2048]{2,1,0:T(4,128)(2,1)} custom-call(s32[4]{0:T(128)S(1)} %copy-done.1, bf16[16,48,512]{2,1,0:T(8,128)(2,1)S(1)} %all_to_all.10.got_ref), custom_call_target="tpu_custom_call" | custom-call | tf_op jit(solution)/shard_map/collect/pallas_call | solution.py:275
  (1 shorter events, 0.0 us)
Async XLA Ops:
  2.8 10.5 %copy-start.3 = (s32[4,12]{1,0:T(4,128)S(1)}, s32[4,12]{1,0:T(4,128)}, u32[]{:S(2)}) copy-start(s32[4,12]{1,0:T(4,128)} %param.11) | copy-start | bytes 580
  2.8 10.7 %copy-start.2 = (bf16[4,12,576]{2,0,1:T(4,128)(2,1)S(1)}, bf16[4,12,576]{2,0,1:T(4,128)(2,1)}, u32[]{:S(2)}) copy-start(bf16[4,12,576]{2,0,1:T(4,128)(2,1)} %param.15) | copy-start | bytes 165892
  2.8 11.1 %copy-start.1 = (s32[4]{0:T(128)S(1)}, s32[4]{0:T(128)}, u32[]{:S(2)}) copy-start(s32[4]{0:T(128)} %owners_ref.3) | copy-start | bytes 52
  2.8 11.1 %copy-start.4 = (s32[4]{0:T(128)S(1)}, s32[4]{0:T(128)}, u32[]{:S(2)}) copy-start(s32[4]{0:T(128)} %param.9) | copy-start | bytes 52
  2.9 27.0 %all-to-all-start = ((bf16[16,48,640]{2,1,0:T(8,128)(2,1)}), bf16[16,48,640]{2,1,0:T(8,128)(2,1)S(1)}, u32[]{:S(2)}, u32[]{:S(2)}) async-start(bf16[16,48,640]{2,1,0:T(8,128)(2,1)} %absorb.1), calls=%async_computation | async-start | bytes 1966080 | tf_op jit(solution)/shard_map/all_to_all | solution.py:235
  14.6 2.2 %copy-start = (bf16[1,3584,576]{1,2,0:T(8,128)(2,1)S(1)}, bf16[1,3584,576]{1,2,0:T(8,128)(2,1)}, u32[]{:S(2)}) copy-start(bf16[1,3584,576]{1,2,0:T(8,128)(2,1)} %param.8) | copy-start | bytes 12386308

commit v4 on v3

--- a/solution.py
+++ b/solution.py
@@ -12,7 +12,7 @@
 ROPE = 64
 NOPE = 128
 NEW_PAD = 128
-CHUNK = 512
+CHUNK = 1024
 HEAD = NEW_PAD + CHUNK
 F32 = jnp.float32
 BF16 = jnp.bfloat16
@@ -83,10 +83,9 @@
     return mine
 
 
-def stage_kernel(strags, info_ref, new_ref, keys_ref, out_ref, tail_ref, hidden, sems):
+def stage_kernel(strags, info_ref, new_ref, keys_ref, out_ref, hidden, sems):
     mine = straggler_here(strags, info_ref)
     width = keys_ref.shape[0]
-    spare = WIDE - width
     count = out_ref.shape[1] - NEW_PAD
 
     @pl.when(mine >= 0)
@@ -96,30 +95,28 @@
                 keys_ref.at[:, pl.ds(0, count)], out_ref.at[pl.ds(0, width), pl.ds(NEW_PAD, count)], sems.at[0]
             ),
             pltpu.make_async_copy(new_ref.at[mine], out_ref.at[:, pl.ds(0, NEW_PAD)], sems.at[1]),
-            pltpu.make_async_copy(
-                hidden.at[:, pl.ds(0, count)], out_ref.at[pl.ds(width, spare), pl.ds(NEW_PAD, count)], sems.at[2]
-            ),
-            pltpu.make_async_copy(hidden, tail_ref, sems.at[3]),
+            pltpu.make_async_copy(hidden, out_ref.at[pl.ds(width, WIDE - width), pl.ds(NEW_PAD, count)], sems.at[2]),
         ]
         copies[0].start()
         copies[1].start()
         length = info_ref[1 + strags + mine]
         hidden[...] = jnp.where(iota2(hidden.shape, 1) < length, 0.0, HIDDEN).astype(BF16)
         copies[2].start()
-        copies[3].start()
         for copy in copies:
             copy.wait()
 
 
-def attend_kernel(strags, info_ref, query_ref, head_ref, tail_ref, keys_ref, out_ref, keys, raw_even, raw_odd, acc, total, top_even, top_odd, key_sems, tail_sem):
+def attend_kernel(strags, info_ref, query_ref, head_ref, keys_ref, out_ref, keys, raw_even, raw_odd, acc, total, top_even, top_odd, key_sems):
     mine = straggler_here(strags, info_ref)
     width, ctx = keys_ref.shape
-    count = ctx // CHUNK
+    first = head_ref.shape[1] - NEW_PAD
+    late = [(at, min(CHUNK, ctx - first - at)) for at in range(0, ctx - first, CHUNK)]
     factor = math.log2(math.e) / math.sqrt(NOPE + ROPE)
 
     def key_copy(i):
-        part = pl.ds(pl.multiple_of(i * CHUNK, CHUNK), CHUNK)
-        return pltpu.make_async_copy(keys_ref.at[:, part], keys.at[pl.ds(0, width), part], key_sems.at[i])
+        at, size = late[i]
+        source, target = pl.ds(first + at, size), pl.ds(at, size)
+        return pltpu.make_async_copy(keys_ref.at[:, source], keys.at[pl.ds(0, width), target], key_sems.at[i])
 
     def score(keys_part, raw, top):
         part = jnp.dot(query_ref[...], keys_part, preferred_element_type=F32)
@@ -150,37 +147,33 @@
 
     def step(keys_next, raw_next, top_next, values_now, raw_now, top_now, size_now, start):
         top = top_now[...]
-        shift = top * factor
-        fade = None if start else jnp.exp2(top_next[...] * factor - shift)
-        pieces = weights(raw_now, size_now, shift)
+        before = None if start else top_next[...]
         if keys_next is not None:
             top_next[...] = score(keys_next, raw_next, top)
+        shift = top * factor
+        fade = None if start else jnp.exp2(before * factor - shift)
+        pieces = weights(raw_now, size_now, shift)
         gather(pieces, values_now, fade)
 
     @pl.when(mine >= 0)
     def _():
-        masks = pltpu.make_async_copy(tail_ref, keys.at[pl.ds(width, WIDE - width)], tail_sem)
-        masks.start()
-        for i in range(count):
+        for i in range(len(late)):
             key_copy(i).start()
-
-        def cached(i, depth):
-            return keys[:depth, pl.ds(pl.multiple_of(i * CHUNK, CHUNK), CHUNK)]
-
-        top_odd[...] = score(head_ref[:, :NEW_PAD], raw_odd, None)
-        step(head_ref[:, NEW_PAD:], raw_even, top_even, head_ref[:KVL, :NEW_PAD], raw_odd, top_odd, NEW_PAD, True)
-        masks.wait()
-        key_copy(0).wait()
-
-        @pl.loop(0, count // 2)
-        def _(pair):
-            i = pair * 2
-            key_copy(i + 1).wait()
-            key_copy(i + 2).wait()
-            step(cached(i + 1, WIDE), raw_odd, top_odd, cached(i, KVL), raw_even, top_even, CHUNK, False)
-            step(cached(i + 2, WIDE), raw_even, top_even, cached(i + 1, KVL), raw_odd, top_odd, CHUNK, False)
-
-        step(None, None, top_odd, cached(count - 1, KVL), raw_even, top_even, CHUNK, False)
+        length = info_ref[1 + strags + mine]
+        spare = (WIDE - width, ctx - first)
+        keys[width:, :] = jnp.where(first + iota2(spare, 1) < length, 0.0, HIDDEN).astype(BF16)
+
+        now, after = (raw_odd, top_odd), (raw_even, top_even)
+        now[1][...] = score(head_ref[:, :NEW_PAD], now[0], None)
+        step(head_ref[:, NEW_PAD:], *after, head_ref[:KVL, :NEW_PAD], *now, NEW_PAD, True)
+        values, held = head_ref[:KVL, NEW_PAD:], first
+        for i, (at, size) in enumerate(late):
+            now, after = after, now
+            key_copy(i).wait()
+            step(keys[:, at : at + size], *after, values, *now, held, False)
+            values, held = keys[:KVL, at : at + size], size
+        now, after = after, now
+        step(None, None, after[1], values, *now, held, False)
         inverse = 1.0 / jnp.sum(total[...], axis=1, keepdims=True)
         out_ref[...] = (acc[...] * inverse).astype(BF16)
 
@@ -242,35 +235,35 @@
     fresh = jnp.concatenate([fresh, unused], axis=2)
     keys = jnp.transpose(cache[0])
     info = jnp.concatenate([me, owners, lengths])
-    staged, masks = pl.pallas_call(
+    staged = pl.pallas_call(
         functools.partial(stage_kernel, strags),
-        out_shape=[jax.ShapeDtypeStruct((WIDE, HEAD), BF16), jax.ShapeDtypeStruct((WIDE - width, ctx), BF16)],
+        out_shape=jax.ShapeDtypeStruct((WIDE, HEAD), BF16),
         in_specs=[smem, anyspace, anyspace],
-        out_specs=[anyspace, anyspace],
-        scratch_shapes=[VMEM((WIDE - width, ctx), BF16), pltpu.SemaphoreType.DMA((4,))],
+        out_specs=anyspace,
+        scratch_shapes=[VMEM((WIDE - width, HEAD - NEW_PAD), BF16), pltpu.SemaphoreType.DMA((3,))],
         compiler_params=pltpu.CompilerParams(vmem_limit_bytes=24 * 2**20),
         cost_estimate=pl.CostEstimate(flops=0, bytes_accessed=4 * WIDE * HEAD, transcendentals=0),
         name="stage",
     )(info, fresh, keys)
+    late = ctx - (HEAD - NEW_PAD)
     answer = pl.pallas_call(
         functools.partial(attend_kernel, strags),
         out_shape=jax.ShapeDtypeStruct((rows, KVL), BF16),
-        in_specs=[smem, vmem, vmem, anyspace, anyspace],
+        in_specs=[smem, vmem, vmem, anyspace],
         out_specs=vmem,
         scratch_shapes=[
-            VMEM((WIDE, ctx), BF16),
+            VMEM((WIDE, late), BF16),
             VMEM((rows, CHUNK), F32),
             VMEM((rows, CHUNK), F32),
             VMEM((rows, KVL), F32),
             VMEM((rows, 128), F32),
             VMEM((rows, 128), F32),
             VMEM((rows, 128), F32),
-            pltpu.SemaphoreType.DMA((ctx // CHUNK,)),
-            pltpu.SemaphoreType.DMA,
+            pltpu.SemaphoreType.DMA((pl.cdiv(late, CHUNK),)),
         ],
         compiler_params=pltpu.CompilerParams(vmem_limit_bytes=48 * 2**20),
         name="attend",
-    )(info, query, staged, masks, keys)
+    )(info, query, staged, keys)
     got = lax.all_to_all(answer.reshape(ranks, per, KVL), "seq", split_axis=0, concat_axis=0, tiled=True)
     out = pl.pallas_call(
         functools.partial(collect_kernel, strags, toks, heads),

time: 60.4 us -> 59.3 us (0.982)
  blocking collectives: 28 us -> 27 us
    all_to_all x1, blocking collectives: 28 us -> 27 us  [shards(): lax.all_to_all(answer.reshape(ranks, per, KVL), 'seq', split_axis=0, conc...]
where the time goes in v4:
time: 59.3 us; the launch traced here: 59 us
  blocking collectives  27 us (46%)
  waiting for transfers between devices  12.5 us (21%)
  starting transfers between devices  10.5 us (18%)
  Pallas kernels  5.44 us (9%)
  local copies, waits for them, and re-layouts  2.8 us (5%)
  other arithmetic  0.64 us (1%)
    all_to_all x1, blocking collectives, shards(): lax.all_to_all(answer.reshape(ranks, per, KVL), 'seq', split_axis=0, conc...  27 us
    all_to_all x1, waiting for transfers between devices, shards(): lax.all_to_all(sending, 'seq', split_axis=0, concat_axis=0, tiled=True)  12.5 us
    all_to_all x1, starting transfers between devices, shards(): lax.all_to_all(sending, 'seq', split_axis=0, concat_axis=0, tiled=True)  10.5 us
    pallas_call x1, Pallas kernels, shards(): pl.pallas_call(functools.partial(absorb_kernel, strags, toks, heads), out...  2.81 us
    unnamed x11, local copies, waits for them, and re-layouts  2.28 us
    pallas_call x1, Pallas kernels, shards(): pl.pallas_call(functools.partial(collect_kernel, strags, toks, heads), ou...  1.48 us
  transfers between devices with their start and end apart: 1, of which 1 were waited for; matrix products, arithmetic and copies ran while one was open for 2% of the time, Pallas kernels for 1%

profile of v4, /device:TPU:1, one launch (start us, length us, event | category | flops | bytes accessed | tf_op | source)
XLA Modules:
  0.0 59.0 jit_solution(14828717240542411035)
XLA Ops:
  0.0 2.8 %absorb.1 = bf16[16,48,640]{2,1,0:T(8,128)(2,1)} custom-call(s32[4]{0:T(128)} %owners_ref.3, bf16[12,4,512]{2,1,0:T(4,128)(2,1)} %bitcast.17, bf16[12,4,256]{2,1,0:T(4,128)(2,1)} %bitcast.18, bf16[512,512]{1,0:T(8,128)(2,1)} %bitcast.15), custom_call_target="tpu_custom_call" | custom-call | tf_op jit(solution)/shard_map/absorb/pallas_call | solution.py:205
  2.8 0.0 copy-start.3
  2.8 0.0 copy-start.2
  2.8 0.0 copy-start.1
  2.9 0.0 copy-start.4
  2.9 10.5 %all-to-all-start = ((bf16[16,48,640]{2,1,0:T(8,128)(2,1)}), bf16[16,48,640]{2,1,0:T(8,128)(2,1)S(1)}, u32[]{:S(2)}, u32[]{:S(2)}) async-start(bf16[16,48,640]{2,1,0:T(8,128)(2,1)} %absorb.1), calls=%async_computation | async-start | bytes 1966080 | tf_op jit(solution)/shard_map/all_to_all | solution.py:228
  13.3 0.0 copy-done.3
  13.3 0.1 copy.10
  13.4 0.1 select_convert_fusion
  13.5 0.0 copy-done.2
  13.5 0.1 pad_maximum_fusion
  13.6 0.4 copy.11
  14.0 0.0 copy-done.1
  14.0 0.0 copy-done.4
  14.0 0.1 pad_add_fusion.info_ref
  14.1 0.2 broadcast_in_dim.28
  14.2 0.4 fusion.1.new_ref
  14.6 0.0 copy-start
  14.6 2.2 %copy-done = bf16[1,3584,576]{1,2,0:T(8,128)(2,1)S(1)} copy-done((bf16[1,3584,576]{1,2,0:T(8,128)(2,1)S(1)}, bf16[1,3584,576]{1,2,0:T(8,128)(2,1)}, u32[]{:S(2)}) %copy-start) | copy-done | bytes 4128792
  16.8 0.6 stage.1.head_ref
  17.4 12.5 %all-to-all-done = bf16[16,48,640]{2,1,0:T(8,128)(2,1)S(1)} async-done(((bf16[16,48,640]{2,1,0:T(8,128)(2,1)}), bf16[16,48,640]{2,1,0:T(8,128)(2,1)S(1)}, u32[]{:S(2)}, u32[]{:S(2)}) %all-to-all-start) | async-done | bytes 983072 | tf_op jit(solution)/shard_map/all_to_all | solution.py:228
  29.9 0.6 attend.1
  30.5 27.0 %all_to_all.10.got_ref = bf16[16,48,512]{2,1,0:T(8,128)(2,1)S(1)} all-to-all(bf16[16,48,512]{2,1,0:T(8,128)(2,1)S(1)} %bitcast.14), channel_id=1, replica_groups=mesh['grp'=32,'seq'=16] {'seq'}, dimensions={0} | all-to-all | bytes 1572864 | tf_op jit(solution)/shard_map/all_to_all | solution.py:267
  57.5 1.5 %collect.1 = bf16[12,4,2048]{2,1,0:T(4,128)(2,1)} custom-call(s32[4]{0:T(128)S(1)} %copy-done.1, bf16[16,48,512]{2,1,0:T(8,128)(2,1)S(1)} %all_to_all.10.got_ref), custom_call_target="tpu_custom_call" | custom-call | tf_op jit(solution)/shard_map/collect/pallas_call | solution.py:268
  (1 shorter events, 0.0 us)
Async XLA Ops:
  2.8 10.5 %copy-start.3 = (s32[4,12]{1,0:T(4,128)S(1)}, s32[4,12]{1,0:T(4,128)}, u32[]{:S(2)}) copy-start(s32[4,12]{1,0:T(4,128)} %param.11) | copy-start | bytes 580
  2.8 10.7 %copy-start.2 = (bf16[4,12,576]{2,0,1:T(4,128)(2,1)S(1)}, bf16[4,12,576]{2,0,1:T(4,128)(2,1)}, u32[]{:S(2)}) copy-start(bf16[4,12,576]{2,0,1:T(4,128)(2,1)} %param.15) | copy-start | bytes 165892
  2.8 11.1 %copy-start.1 = (s32[4]{0:T(128)S(1)}, s32[4]{0:T(128)}, u32[]{:S(2)}) copy-start(s32[4]{0:T(128)} %owners_ref.3) | copy-start | bytes 52
  2.9 11.1 %copy-start.4 = (s32[4]{0:T(128)S(1)}, s32[4]{0:T(128)}, u32[]{:S(2)}) copy-start(s32[4]{0:T(128)} %param.9) | copy-start | bytes 52
  2.9 27.0 %all-to-all-start = ((bf16[16,48,640]{2,1,0:T(8,128)(2,1)}), bf16[16,48,640]{2,1,0:T(8,128)(2,1)S(1)}, u32[]{:S(2)}, u32[]{:S(2)}) async-start(bf16[16,48,640]{2,1,0:T(8,128)(2,1)} %absorb.1), calls=%async_computation | async-start | bytes 1966080 | tf_op jit(solution)/shard_map/all_to_all | solution.py:228
  14.6 2.2 %copy-start = (bf16[1,3584,576]{1,2,0:T(8,128)(2,1)S(1)}, bf16[1,3584,576]{1,2,0:T(8,128)(2,1)}, u32[]{:S(2)}) copy-start(bf16[1,3584,576]{1,2,0:T(8,128)(2,1)} %param.8) | copy-start | bytes 12386308

commit v5 on v4

--- a/solution.py
+++ b/solution.py
@@ -12,8 +12,8 @@
 ROPE = 64
 NOPE = 128
 NEW_PAD = 128
-CHUNK = 1024
-HEAD = NEW_PAD + CHUNK
+CHUNK = 512
+HEAD = NEW_PAD + 2 * CHUNK
 F32 = jnp.float32
 BF16 = jnp.bfloat16
 HIDDEN = -1e30
@@ -110,12 +110,12 @@
     mine = straggler_here(strags, info_ref)
     width, ctx = keys_ref.shape
     first = head_ref.shape[1] - NEW_PAD
-    late = [(at, min(CHUNK, ctx - first - at)) for at in range(0, ctx - first, CHUNK)]
+    count = (ctx - first) // CHUNK
     factor = math.log2(math.e) / math.sqrt(NOPE + ROPE)
 
     def key_copy(i):
-        at, size = late[i]
-        source, target = pl.ds(first + at, size), pl.ds(at, size)
+        source = pl.ds(pl.multiple_of(first + i * CHUNK, CHUNK), CHUNK)
+        target = pl.ds(pl.multiple_of(i * CHUNK, CHUNK), CHUNK)
         return pltpu.make_async_copy(keys_ref.at[:, source], keys.at[pl.ds(0, width), target], key_sems.at[i])
 
     def score(keys_part, raw, top):
@@ -157,36 +157,43 @@
 
     @pl.when(mine >= 0)
     def _():
-        for i in range(len(late)):
+        for i in range(count):
             key_copy(i).start()
         length = info_ref[1 + strags + mine]
         spare = (WIDE - width, ctx - first)
         keys[width:, :] = jnp.where(first + iota2(spare, 1) < length, 0.0, HIDDEN).astype(BF16)
 
-        now, after = (raw_odd, top_odd), (raw_even, top_even)
-        now[1][...] = score(head_ref[:, :NEW_PAD], now[0], None)
-        step(head_ref[:, NEW_PAD:], *after, head_ref[:KVL, :NEW_PAD], *now, NEW_PAD, True)
-        values, held = head_ref[:KVL, NEW_PAD:], first
-        for i, (at, size) in enumerate(late):
-            now, after = after, now
-            key_copy(i).wait()
-            step(keys[:, at : at + size], *after, values, *now, held, False)
-            values, held = keys[:KVL, at : at + size], size
-        now, after = after, now
-        step(None, None, after[1], values, *now, held, False)
+        def cached(i, depth):
+            return keys[:depth, pl.ds(pl.multiple_of(i * CHUNK, CHUNK), CHUNK)]
+
+        second = NEW_PAD + CHUNK
+        top_odd[...] = score(head_ref[:, :NEW_PAD], raw_odd, None)
+        step(head_ref[:, NEW_PAD:second], raw_even, top_even, head_ref[:KVL, :NEW_PAD], raw_odd, top_odd, NEW_PAD, True)
+        step(head_ref[:, second:], raw_odd, top_odd, head_ref[:KVL, NEW_PAD:second], raw_even, top_even, CHUNK, False)
+        key_copy(0).wait()
+        step(cached(0, WIDE), raw_even, top_even, head_ref[:KVL, second:], raw_odd, top_odd, CHUNK, False)
+
+        @pl.loop(0, count // 2)
+        def _(pair):
+            i = pair * 2
+            key_copy(i + 1).wait()
+            step(cached(i + 1, WIDE), raw_odd, top_odd, cached(i, KVL), raw_even, top_even, CHUNK, False)
+            key_copy(i + 2).wait()
+            step(cached(i + 2, WIDE), raw_even, top_even, cached(i + 1, KVL), raw_odd, top_odd, CHUNK, False)
+
+        step(None, None, top_odd, cached(count - 1, KVL), raw_even, top_even, CHUNK, False)
         inverse = 1.0 / jnp.sum(total[...], axis=1, keepdims=True)
         out_ref[...] = (acc[...] * inverse).astype(BF16)
 
 
-def collect_kernel(strags, toks, heads, owners_ref, got_ref, out_ref, held):
+def collect_kernel(strags, toks, heads, owners_ref, got_ref, out_ref):
     per = toks * heads
-    for s in range(strags):
-        held[s * per : (s + 1) * per, :] = got_ref[owners_ref[s]]
+    held = jnp.concatenate([got_ref[owners_ref[s]] for s in range(strags)], axis=0)
     shape = (toks * strags, strags * per)
     row, col = iota2(shape, 0), iota2(shape, 1)
     for h in range(heads):
         pick = (col == row % strags * per + row // strags * heads + h).astype(F32).astype(BF16)
-        lined = jnp.dot(pick, held[...], preferred_element_type=F32).astype(BF16)
+        lined = jnp.dot(pick, held, preferred_element_type=F32).astype(BF16)
         for t in range(toks):
             out_ref[t, :, h * KVL : (h + 1) * KVL] = lined[t * strags : (t + 1) * strags]
 
@@ -259,7 +266,7 @@
             VMEM((rows, 128), F32),
             VMEM((rows, 128), F32),
             VMEM((rows, 128), F32),
-            pltpu.SemaphoreType.DMA((pl.cdiv(late, CHUNK),)),
+            pltpu.SemaphoreType.DMA((late // CHUNK,)),
         ],
         compiler_params=pltpu.CompilerParams(vmem_limit_bytes=48 * 2**20),
         name="attend",
@@ -270,7 +277,6 @@
         out_shape=jax.ShapeDtypeStruct((toks, strags, heads * KVL), BF16),
         in_specs=[smem, vmem],
         out_specs=vmem,
-        scratch_shapes=[VMEM((strags * per, KVL), BF16)],
         compiler_params=pltpu.CompilerParams(vmem_limit_bytes=32 * 2**20),
         name="collect",
     )(owners, got)

time: 59.3 us -> 59.2 us (level)
  no operation moved by 1% of the time
where the time goes in v5:
time: 59.2 us; the launch traced here: 59 us
  blocking collectives  27 us (46%)
  waiting for transfers between devices  12.5 us (21%)
  starting transfers between devices  10.5 us (18%)
  Pallas kernels  5.44 us (9%)
  local copies, waits for them, and re-layouts  2.8 us (5%)
  other arithmetic  0.64 us (1%)
    all_to_all x1, blocking collectives, shards(): lax.all_to_all(answer.reshape(ranks, per, KVL), 'seq', split_axis=0, conc...  27 us
    all_to_all x1, waiting for transfers between devices, shards(): lax.all_to_all(sending, 'seq', split_axis=0, concat_axis=0, tiled=True)  12.5 us
    all_to_all x1, starting transfers between devices, shards(): lax.all_to_all(sending, 'seq', split_axis=0, concat_axis=0, tiled=True)  10.5 us
    pallas_call x1, Pallas kernels, shards(): pl.pallas_call(functools.partial(absorb_kernel, strags, toks, heads), out...  2.79 us
    unnamed x11, local copies, waits for them, and re-layouts  2.28 us
    pallas_call x1, Pallas kernels, shards(): pl.pallas_call(functools.partial(collect_kernel, strags, toks, heads), ou...  1.48 us
  transfers between devices with their start and end apart: 1, of which 1 were waited for; matrix products, arithmetic and copies ran while one was open for 2% of the time, Pallas kernels for 1%

profile of v5, /device:TPU:1, one launch (start us, length us, event | category | flops | bytes accessed | tf_op | source)
XLA Modules:
  0.0 59.0 jit_solution(9590043986085510107)
XLA Ops:
  0.0 2.8 %absorb.1 = bf16[16,48,640]{2,1,0:T(8,128)(2,1)} custom-call(s32[4]{0:T(128)} %owners_ref.3, bf16[12,4,512]{2,1,0:T(4,128)(2,1)} %bitcast.17, bf16[12,4,256]{2,1,0:T(4,128)(2,1)} %bitcast.18, bf16[512,512]{1,0:T(8,128)(2,1)} %bitcast.15), custom_call_target="tpu_custom_call" | custom-call | tf_op jit(solution)/shard_map/absorb/pallas_call | solution.py:212
  2.8 0.0 copy-start.3
  2.8 0.0 copy-start.2
  2.8 0.0 copy-start.1
  2.8 0.0 copy-start.4
  2.8 10.5 %all-to-all-start = ((bf16[16,48,640]{2,1,0:T(8,128)(2,1)}), bf16[16,48,640]{2,1,0:T(8,128)(2,1)S(1)}, u32[]{:S(2)}, u32[]{:S(2)}) async-start(bf16[16,48,640]{2,1,0:T(8,128)(2,1)} %absorb.1), calls=%async_computation | async-start | bytes 1966080 | tf_op jit(solution)/shard_map/all_to_all | solution.py:235
  13.3 0.0 copy-done.3
  13.3 0.1 copy.10
  13.4 0.1 select_convert_fusion
  13.5 0.0 copy-done.2
  13.5 0.1 pad_maximum_fusion
  13.6 0.4 copy.11
  13.9 0.0 copy-done.1
  14.0 0.0 copy-done.4
  14.0 0.1 pad_add_fusion.info_ref
  14.0 0.2 broadcast_in_dim.28
  14.2 0.4 fusion.1.new_ref
  14.6 0.0 copy-start
  14.6 2.2 %copy-done = bf16[1,3584,576]{1,2,0:T(8,128)(2,1)S(1)} copy-done((bf16[1,3584,576]{1,2,0:T(8,128)(2,1)S(1)}, bf16[1,3584,576]{1,2,0:T(8,128)(2,1)}, u32[]{:S(2)}) %copy-start) | copy-done | bytes 4128792
  16.8 0.6 stage.1.head_ref
  17.4 12.5 %all-to-all-done = bf16[16,48,640]{2,1,0:T(8,128)(2,1)S(1)} async-done(((bf16[16,48,640]{2,1,0:T(8,128)(2,1)}), bf16[16,48,640]{2,1,0:T(8,128)(2,1)S(1)}, u32[]{:S(2)}, u32[]{:S(2)}) %all-to-all-start) | async-done | bytes 983072 | tf_op jit(solution)/shard_map/all_to_all | solution.py:235
  29.9 0.6 %attend.1 = bf16[768,512]{1,0:T(8,128)(2,1)S(1)} custom-call(s32[9]{0:T(128)S(1)} %pad_add_fusion.info_ref, bf16[768,640]{1,0:T(8,128)(2,1)S(1)} %bitcast.13, bf16[640,1152]{1,0:T(8,128)(2,1)S(1)} %stage.1.head_ref, bf16[576,3584]{1,0:T(8,128)(2,1)} %bitcast.11), custom_call_target="tpu_custom_call" | custom-call | tf_op jit(solution)/shard_map/attend/pallas_call | solution.py:256
  30.5 27.0 %all_to_all.10.got_ref = bf16[16,48,512]{2,1,0:T(8,128)(2,1)S(1)} all-to-all(bf16[16,48,512]{2,1,0:T(8,128)(2,1)S(1)} %bitcast.14), channel_id=1, replica_groups=mesh['grp'=32,'seq'=16] {'seq'}, dimensions={0} | all-to-all | bytes 1572864 | tf_op jit(solution)/shard_map/all_to_all | solution.py:274
  57.5 1.5 %collect.1 = bf16[12,4,2048]{2,1,0:T(4,128)(2,1)} custom-call(s32[4]{0:T(128)S(1)} %copy-done.1, bf16[16,48,512]{2,1,0:T(8,128)(2,1)S(1)} %all_to_all.10.got_ref), custom_call_target="tpu_custom_call" | custom-call | tf_op jit(solution)/shard_map/collect/pallas_call | solution.py:275
  (1 shorter events, 0.0 us)
Async XLA Ops:
  2.8 10.5 %copy-start.3 = (s32[4,12]{1,0:T(4,128)S(1)}, s32[4,12]{1,0:T(4,128)}, u32[]{:S(2)}) copy-start(s32[4,12]{1,0:T(4,128)} %param.11) | copy-start | bytes 580
  2.8 10.7 %copy-start.2 = (bf16[4,12,576]{2,0,1:T(4,128)(2,1)S(1)}, bf16[4,12,576]{2,0,1:T(4,128)(2,1)}, u32[]{:S(2)}) copy-start(bf16[4,12,576]{2,0,1:T(4,128)(2,1)} %param.15) | copy-start | bytes 165892
  2.8 11.1 %copy-start.1 = (s32[4]{0:T(128)S(1)}, s32[4]{0:T(128)}, u32[]{:S(2)}) copy-start(s32[4]{0:T(128)} %owners_ref.3) | copy-start | bytes 52
  2.8 11.1 %copy-start.4 = (s32[4]{0:T(128)S(1)}, s32[4]{0:T(128)}, u32[]{:S(2)}) copy-start(s32[4]{0:T(128)} %param.9) | copy-start | bytes 52
  2.8 27.0 %all-to-all-start = ((bf16[16,48,640]{2,1,0:T(8,128)(2,1)}), bf16[16,48,640]{2,1,0:T(8,128)(2,1)S(1)}, u32[]{:S(2)}, u32[]{:S(2)}) async-start(bf16[16,48,640]{2,1,0:T(8,128)(2,1)} %absorb.1), calls=%async_computation | async-start | bytes 1966080 | tf_op jit(solution)/shard_map/all_to_all | solution.py:235
  14.6 2.2 %copy-start = (bf16[1,3584,576]{1,2,0:T(8,128)(2,1)S(1)}, bf16[1,3584,576]{1,2,0:T(8,128)(2,1)}, u32[]{:S(2)}) copy-start(bf16[1,3584,576]{1,2,0:T(8,128)(2,1)} %param.8) | copy-start | bytes 12386308
